TPU v7x, 128 devices: a whole 4x4x4 slice. The times are simulated.
128 devices in a mesh: fsdp: 8 (over x_lo, z), ctx: 16 (over x_hi, y, core).
Axes of the slice: x: 4 (x_hi: 2, x_lo: 2; x = x_hi * 2 + x_lo), y: 4, z: 4, core: 2. Of those that a mesh axis runs over, the one named last changes fastest.
Arguments:
- streams: bfloat16 [8, 4096, 12288], P('fsdp', 'ctx'), may hold values from -6 to 6
- cotangent: bfloat16 [8, 4096, 4096], P('fsdp', 'ctx'), may hold values from -6 to 6
- filters: float32 [256, 128], P(('fsdp', 'ctx')), may hold values from -0.54 to 0.54
- short_taps: float32 [3, 12288], P(None, ('fsdp', 'ctx')), may hold values from -3.6 to 3.6
Outputs:
- result: bfloat16 [8, 4096, 4096], P('fsdp', 'ctx')
- stream_grad: bfloat16 [8, 4096, 12288], P('fsdp', 'ctx')
- filter_grad: float32 [256, 128], P(('fsdp', 'ctx'))
- short_grad: float32 [3, 12288], P(None, ('fsdp', 'ctx'))
All inputs are finite; a program needn't handle non-finite values.
Results may differ from a plain program's by a relative error of at most 0.0076.
Values may be sent and summed in bfloat16 or wider, within the bound.
No kernel may reach another device: no remote copies, remote signals or barrier semaphores. Data moves between devices by JAX's collectives and lax.ppermute only.
A program may use at most 256 MiB of HBM per device.

v0:
```python
import math

import jax
import jax.numpy as jnp
import numpy as np
from jax import lax
from jax.sharding import PartitionSpec as P


def shifted(value, axis, by):
    length = lax.axis_size(axis)
    pairs = [(i, i + by) for i in range(length) if 0 <= i + by < length]
    return lax.ppermute(value, axis, pairs)


def build_kernels(filters, tap_count):
    narrow = filters.astype(jnp.bfloat16)
    row_index = np.arange(tap_count)[:, None]
    col_index = np.arange(2 * tap_count)[None, :]
    kernels = []
    for lag_table in (row_index + tap_count - col_index, col_index - row_index):
        usable = (lag_table >= 0) & (lag_table < tap_count)
        picked = narrow[:, np.clip(lag_table, 0, tap_count - 1)]
        kernels.append(jnp.where(usable[None], picked, jnp.zeros((), jnp.bfloat16)))
    return (kernels[0], kernels[1])


def block_pairs(padded, tap_count):
    channels = padded.shape[0]
    col_total = padded.shape[1] - tap_count
    block_count = col_total // tap_count
    leading = padded[:, :col_total].reshape(channels, block_count, tap_count)
    trailing = padded[:, tap_count:].reshape(channels, block_count, tap_count)
    return jnp.concatenate([leading, trailing], axis=2)


def apply_kernel(kernel, paired, group_count):
    channels, block_count, span_cols = paired.shape
    grouped = paired.reshape(group_count, channels // group_count, block_count, span_cols)
    mapped = jnp.einsum("gij,gcbj->gcbi", kernel, grouped, preferred_element_type=jnp.float32)
    return mapped.reshape(channels, block_count * kernel.shape[1])


def diagonal_sums(moment, tap_count):
    row_index = np.arange(tap_count)[:, None]
    lag_index = np.arange(tap_count)[None, :]
    picked = moment[:, row_index, row_index + tap_count - lag_index]
    return jnp.sum(picked, axis=1)


def featurize(window, whole_taps):
    return (
        whole_taps[0][:, None] * window[:, 2:]
        + whole_taps[1][:, None] * window[:, 1:-1]
        + whole_taps[2][:, None] * window[:, :-2]
    ).astype(jnp.bfloat16)


def gate_product(feats, channels):
    return (
        feats[:channels].astype(jnp.float32) * feats[2 * channels :].astype(jnp.float32)
    ).astype(jnp.bfloat16)


def on_device(streams, cotangent, filters, short_taps):
    stream = streams[0].T
    grad_out = cotangent[0].T
    row_count = stream.shape[1]
    channels = grad_out.shape[0]
    whole_filters, whole_taps = (
        lax.all_gather(filters, ("fsdp", "ctx"), axis=0, tiled=True),
        lax.all_gather(short_taps, ("fsdp", "ctx"), axis=1, tiled=True),
    )
    group_count = whole_filters.shape[0]
    tap_count = whole_filters.shape[1]
    earlier = shifted(stream[:, row_count - 2 :], "ctx", 1)
    extended = jnp.concatenate([earlier, stream], axis=1)
    feats = featurize(extended, whole_taps)
    mixed = gate_product(feats, channels)
    carried = shifted(mixed[:, row_count - tap_count + 1 :], "ctx", 1)
    first = feats[:channels].astype(jnp.float32)
    second = feats[channels : 2 * channels].astype(jnp.float32)
    values = feats[2 * channels :].astype(jnp.float32)
    kernel_ahead, kernel_behind = build_kernels(whole_filters, tap_count)
    padded = jnp.concatenate([jnp.zeros((channels, 1), jnp.bfloat16), carried, mixed], axis=1)
    paired = block_pairs(padded, tap_count)
    hidden = apply_kernel(kernel_ahead, paired, group_count)
    result = (second * hidden).astype(jnp.bfloat16)
    grad_f = grad_out.astype(jnp.float32)
    gated = (grad_f * second).astype(jnp.bfloat16)
    second_grad = grad_f * hidden
    later = shifted(gated[:, : tap_count - 1], "ctx", -1)
    gpadded = jnp.concatenate([gated, later, jnp.zeros((channels, 1), jnp.bfloat16)], axis=1)
    mixed_grad = apply_kernel(kernel_behind, block_pairs(gpadded, tap_count), group_count)
    feat_grad = jnp.concatenate([mixed_grad * values, second_grad, mixed_grad * first], axis=0)
    following = shifted(feat_grad[:, :2], "ctx", -1)
    grad_ext = jnp.concatenate([feat_grad, following], axis=1)
    stream_grad = (
        whole_taps[0][:, None] * feat_grad
        + whole_taps[1][:, None] * grad_ext[:, 1 : row_count + 1]
        + whole_taps[2][:, None] * grad_ext[:, 2 : row_count + 2]
    ).astype(jnp.bfloat16)
    short_part = jnp.stack(
        [
            jnp.sum(
                feat_grad * extended[:, 2 - offset : 2 - offset + row_count].astype(jnp.float32),
                axis=1,
            )
            for offset in range(3)
        ]
    )
    block_count = row_count // tap_count
    gate_blocks = gated.reshape(group_count, channels // group_count, block_count, tap_count)
    mixed_blocks = paired.reshape(group_count, channels // group_count, block_count, 2 * tap_count)
    moment = jnp.einsum(
        "gcbi,gcbj->gij", gate_blocks, mixed_blocks, preferred_element_type=jnp.float32
    )
    filter_part = diagonal_sums(moment, tap_count)
    factor = 1.0 / math.sqrt(lax.axis_size("fsdp") * lax.axis_size("ctx") * row_count)
    filter_grad, short_grad = (
        lax.psum_scatter(filter_part * factor, ("fsdp", "ctx"), scatter_dimension=0, tiled=True),
        lax.psum_scatter(short_part * factor, ("fsdp", "ctx"), scatter_dimension=1, tiled=True),
    )
    return (result.T[None], stream_grad.T[None], filter_grad, short_grad)


def solution(mesh):
    in_specs = (
        P("fsdp", "ctx", None),
        P("fsdp", "ctx", None),
        P(("fsdp", "ctx"), None),
        P(None, ("fsdp", "ctx")),
    )
    out_specs = (
        P("fsdp", "ctx", None),
        P("fsdp", "ctx", None),
        P(("fsdp", "ctx"), None),
        P(None, ("fsdp", "ctx")),
    )
    return jax.shard_map(
        on_device, mesh=mesh, in_specs=in_specs, out_specs=out_specs, check_vma=False
    )
```

profile of v0, /device:TPU:1, one launch (start us, length us, event | category | flops | bytes accessed | tf_op | source)
XLA Modules:
  0.0 1898.3 jit_solution(6605658366686765229)
XLA Ops:
  7.2 8.6 copy.40
  19.6 4.6 collective-permute-start
  24.2 178.2 %all-gather = f32[128,96,3]{1,2,0:T(4,128)S(1)} all-gather(f32[1,96,3]{1,2,0:T(4,128)S(1)} %bitcast.100), channel_id=1, replica_groups=mesh['fsdp'=8,'ctx'=16] {'fsdp','ctx'}, dimensions={0}, use_global_device_ids=true | all-gather | bytes 148608 | tf_op jit(solution)/shard_map/all_gather | solution.py:72
  202.8 4.1 copy.48
  208.5 13.8 fusion.10
  225.1 173.5 %all-gather.1 = bf16[128,2,128]{2,1,0:T(2,128)(2,1)S(1)} all-gather(bf16[1,2,128]{2,1,0:T(2,128)(2,1)S(1)} %bitcast_convert_fusion), channel_id=1, replica_groups=mesh['fsdp'=8,'ctx'=16] {'fsdp','ctx'}, dimensions={0}, use_global_device_ids=true | all-gather | bytes 66048 | tf_op jit(solution)/shard_map/all_gather | solution.py:71
  398.7 129.4 %gather_fusion.1 = bf16[32768,256]{1,0:T(8,128)(2,1)} fusion(bf16[256,128]{0,1:T(8,128)(2,1)S(1)} %copy.45, s32[32768]{0:T(1024)S(1)} %broadcast_clamp_fusion), kind=kCustom, calls=%fused_computation.1 | custom fusion | bytes 33685504 | tf_op jit(solution)/shard_map/gather | solution.py:23
  528.1 23.0 %copy.52 = bf16[128,256,256]{1,0,2:T(8,128)(2,1)} copy(bf16[128,256,256]{2,1,0:T(8,128)(2,1)} %bitcast.82) | data formatting | bytes 33554432 | tf_op jit(solution)/shard_map/gather | solution.py:23
  559.3 4.0 concatenate.41
  565.3 11.2 fusion
  576.5 4.3 copy.53
  580.9 4.3 convert_multiply_fusion.6
  587.9 4.6 collective-permute-start.1
  592.5 129.4 %gather_fusion = bf16[32768,256]{1,0:T(8,128)(2,1)} fusion(bf16[256,128]{0,1:T(8,128)(2,1)S(1)} %copy.45, s32[32768]{0:T(1024)S(1)} %broadcast_clamp_fusion.1), kind=kCustom, calls=%fused_computation | custom fusion | bytes 33685504 | tf_op jit(solution)/shard_map/gather | solution.py:23
  721.9 23.6 %copy.46 = bf16[128,256,256]{1,0,2:T(8,128)(2,1)} copy(bf16[128,256,256]{2,1,0:T(8,128)(2,1)} %bitcast.81) | data formatting | bytes 33554432 | tf_op jit(solution)/shard_map/gather | solution.py:23
  745.5 4.0 concatenate.37
  749.5 3.9 pad_maximum_fusion.5
  753.4 4.0 concatenate.36
  761.8 13.1 convolution_bitcast_fusion
  774.9 9.4 fusion.2
  791.5 11.3 pad_maximum_fusion.1
  805.7 4.4 copy.54
  812.2 35.0 %copy.57 = f32[256,128,256]{0,2,1:T(8,128)} copy(f32[256,128,256]{2,1,0:T(8,128)} %convolution_bitcast_fusion) | data formatting | bytes 67108864 | tf_op jit(solution)/shard_map/gcbi,gcbj->gij/dot_general | solution.py:115
  847.2 260.0 %gather_fusion.2 = f32[16384,256]{1,0:T(8,128)} fusion(f32[256,128,256]{0,2,1:T(8,128)} %copy.57, s32[16384]{0:T(1024)S(1)} %copy-done), kind=kCustom, calls=%fused_computation.2 | custom fusion | bytes 33685504 | tf_op jit(solution)/shard_map/gather | solution.py:47
  1107.2 6.8 reduce
  1114.9 4.3 copy.55
  1119.2 17.6 pad_maximum_fusion
  1136.8 31.5 %fusion.12 = (f32[12288]{0:T(1024)S(1)}, f32[12288]{0:T(1024)S(1)}, f32[12288]{0:T(1024)S(1)}, bf16[1,256,12288]{1,2,0:T(8,128)(2,1)}) fusion(bf16[12288,256]{1,0:T(8,128)(2,1)S(1)} %bitcast.79, bf16[12288,2]{1,0:T(8,128)(2,1)} %copy-done.5, f32[4096,256]{1,0:T(8,128)} %get-tuple-element.17, f32[4096,256]{1,0:T(8,128)} %copy-done.1, ...), kind=kLoop, calls=%fused_computation.23 | loop fusion | flops 72314880 | bytes 56967168 | tf_op jit(solution)/shard_map/reduce_sum | solution.py:105
  1168.4 4.0 copy.64
  1175.4 74.7 %all-reduce.3.cloned.1.call-done = f32[256,128]{1,0:T(8,128)} async-done(((f32[256,128]{1,0:T(8,128)}), f32[256,128]{1,0:T(8,128)}) %all-reduce.3.cloned.1.call-update) | async-done | bytes 131088
  1251.3 8.6 copy.60
  1259.9 629.9 %reduce-scatter.4.cloned.1.call-done = f32[96,3]{1,0:T(8,128)} async-done(((f32[12288,3]{1,0:T(8,128)}), f32[96,3]{1,0:T(8,128)}) %reduce-scatter.4.cloned.1.call-update) | async-done | bytes 1168
  (99 shorter events, 44.4 us)
Async XLA Ops:
  7.2 1242.9 %all-reduce.3.cloned.1.call-start = ((), (), s32[]{:S(2)}) async-start(), calls=%async_computation.2 | async-start | bytes 262144
  15.8 8.4 copy-start.22
  19.6 187.2 %collective-permute-start = (bf16[12288,2]{0,1:T(2,128)(2,1)S(1)}, bf16[12288,2]{0,1:T(2,128)(2,1)S(1)}, u32[]{:S(2)}, u32[]{:S(2)}) collective-permute-start(bf16[12288,2]{0,1:T(2,128)(2,1)S(1)} %copy.41), channel_id=1, source_target_pairs={{0,1},{1,2},{2,3},{3,4},{4,5},{5,6},{6,7},{7,8},{8,9},{9,10},{10,1... | collective-permute-start | bytes 147464 | tf_op jit(solution)/shard_map/ppermute | solution.py:13
  202.7 19.5 %copy-start.12 = (f32[1,12288]{1,0:T(1,128)}, f32[1,12288]{1,0:T(1,128)S(1)}, u32[]{:S(2)}) copy-start(f32[1,12288]{1,0:T(1,128)S(1)} %get-tuple-element.21) | copy-start | bytes 147460
  202.7 19.5 %copy-start.14 = (f32[1,12288]{1,0:T(1,128)}, f32[1,12288]{1,0:T(1,128)S(1)}, u32[]{:S(2)}) copy-start(f32[1,12288]{1,0:T(1,128)S(1)} %get-tuple-element.22) | copy-start | bytes 147460
  202.7 19.5 %copy-start.16 = (f32[1,12288]{1,0:T(1,128)}, f32[1,12288]{1,0:T(1,128)S(1)}, u32[]{:S(2)}) copy-start(f32[1,12288]{1,0:T(1,128)S(1)} %get-tuple-element.23) | copy-start | bytes 147460
  208.4 13.8 copy-start.5
  208.4 13.8 copy-start.9
  222.3 176.3 %copy-start.4 = (bf16[12288,256]{1,0:T(8,128)(2,1)}, bf16[12288,256]{1,0:T(8,128)(2,1)S(1)}, u32[]{:S(2)}) copy-start(bf16[12288,256]{1,0:T(8,128)(2,1)S(1)} %fusion.10) | copy-start | bytes 18874372
  222.3 2.8 copy-start.23
  222.3 176.4 %copy-start.19 = (s32[32768]{0:T(1024)S(1)}, s32[32768]{0:T(1024)}, u32[]{:S(2)}) copy-start(s32[32768]{0:T(1024)} %constant.63) | copy-start | bytes 393220
  222.9 175.7 %copy-start.6 = (bf16[4096,256]{1,0:T(8,128)(2,1)}, bf16[4096,256]{1,0:T(8,128)(2,1)S(1)}, u32[]{:S(2)}) copy-start(bf16[4096,256]{1,0:T(8,128)(2,1)S(1)} %fusion.22) | copy-start | bytes 6291460
  223.0 332.4 %collective-permute-start.2 = (bf16[4096,127]{1,0:T(8,128)(2,1)S(1)}, bf16[4096,127]{1,0:T(8,128)(2,1)}, u32[]{:S(2)}, u32[]{:S(2)}) collective-permute-start(bf16[4096,127]{1,0:T(8,128)(2,1)S(1)} %slice.87), channel_id=1, source_target_pairs={{1,0},{2,1},{3,2},{4,3},{5,4},{6,5},{7,6},{8,7},{9,8},{10,9},{11,1... | collective-permute-start | bytes 3121160 | tf_op jit(solution)/shard_map/ppermute | solution.py:13
  528.1 23.0 %copy-start.21 = (pred[128,256]{1,0:T(32,128)(4,1)S(1)}, pred[128,256]{1,0:T(32,128)(4,1)}, u32[]{:S(2)}) copy-start(pred[128,256]{1,0:T(32,128)(4,1)} %constant.44) | copy-start | bytes 98308
  553.7 2.3 copy-start.7
  563.3 17.6 slice-start.2
  565.3 15.6 slice-start.3
  580.9 11.6 copy-start.18
  587.9 161.7 %collective-permute-start.1 = (bf16[4096,127]{1,0:T(8,128)(2,1)}, bf16[4096,127]{1,0:T(8,128)(2,1)}, u32[]{:S(2)}, u32[]{:S(2)}) collective-permute-start(bf16[4096,127]{1,0:T(8,128)(2,1)} %slice.86), channel_id=1, source_target_pairs={{0,1},{1,2},{2,3},{3,4},{4,5},{5,6},{6,7},{7,8},{8,9},{9,10},{10,1... | collective-permute-start | bytes 3121160 | tf_op jit(solution)/shard_map/ppermute | solution.py:13
  721.9 23.6 %copy-start.20 = (pred[128,256]{1,0:T(32,128)(4,1)S(1)}, pred[128,256]{1,0:T(32,128)(4,1)}, u32[]{:S(2)}) copy-start(pred[128,256]{1,0:T(32,128)(4,1)} %constant.42) | copy-start | bytes 98308
  786.6 3.8 copy-start.2
  786.6 4.9 copy-start.3
  790.4 12.5 copy-start.1
  810.2 37.1 %copy-start = (s32[16384]{0:T(1024)S(1)}, s32[16384]{0:T(1024)}, u32[]{:S(2)}) copy-start(s32[16384]{0:T(1024)} %constant.71) | copy-start | bytes 196612
  810.2 304.7 %collective-permute-start.3 = (f32[12288,2]{0,1:T(2,128)S(1)}, f32[12288,2]{0,1:T(2,128)S(1)}, u32[]{:S(2)}, u32[]{:S(2)}) collective-permute-start(f32[12288,2]{0,1:T(2,128)S(1)} %copy.54), channel_id=1, source_target_pairs={{1,0},{2,1},{3,2},{4,3},{5,4},{6,5},{7,6},{8,7},{9,8},{10,9},{11,1... | collective-permute-start | bytes 294920 | tf_op jit(solution)/shard_map/ppermute | solution.py:13
  1114.8 775.0 %reduce-scatter.4.cloned.1.call-start = ((), (), s32[]{:S(2)}) async-start(), calls=%async_computation.1 | async-start | bytes 6340608
  1114.9 21.9 %slice-start = ((s8[6291456]{0:T(1024)(128)(4,1)}), s8[2097152]{0:T(1024)(128)(4,1)S(1)}, s32[]{:S(2)}) async-start(s8[6291456]{0:T(1024)(128)(4,1)} %bitcast.77), calls=%async_computation.3 | async-start | bytes 4194304
  1119.2 17.6 slice-start.1
  1119.2 17.6 copy-start.13
  1119.2 17.6 copy-start.15
  1119.2 17.6 copy-start.17
  1168.4 4.1 copy-start.11
  (2 other events, 3.5 us)
Sparse Core Ops, SparseCore 0:
  1114.9 135.0 all-reduce.2
  1252.5 637.1 reduce-scatter.3
where the time goes:
time: 1910 us; the launch traced here: 1900 us
  waiting for transfers between devices  705 us (37%)
  local copies, waits for them, and re-layouts  683 us (36%)
  blocking collectives  352 us (18%)
  other arithmetic  97 us (5%)
  matrix products  33.8 us (2%)
    unnamed x4, waiting for transfers between devices  705 us
    gather x4, local copies, waits for them, and re-layouts, build_kernels(): picked = narrow[:, np.clip(lag_table, 0, tap_count - 1)]  305 us
    gather x1, local copies, waits for them, and re-layouts, diagonal_sums(): picked = moment[:, row_index, row_index + tap_count - lag_index]  260 us
    all_gather x1, blocking collectives, on_device(): lax.all_gather(short_taps, ('fsdp', 'ctx'), axis=1, tiled=True)  178 us
    all_gather x1, blocking collectives, on_device(): lax.all_gather(filters, ('fsdp', 'ctx'), axis=0, tiled=True)  173 us
  transfers between devices with their start and end apart: 6, of which 2 were waited for; matrix products, arithmetic and copies ran while one was open for 36% of the time, Pallas kernels for 0%

commit v1 on v0

v1 whole, which is shorter than its diff:
```python
import functools
import math

import jax
import jax.numpy as jnp
import numpy as np
from jax import lax
from jax.experimental import pallas as pl
from jax.experimental.pallas import tpu as pltpu
from jax.sharding import PartitionSpec as P

F32, BF16 = jnp.float32, jnp.bfloat16
LANES = 128
PACK = 16
BLOCK = 32


def shifted(value, axis, by):
    length = lax.axis_size(axis)
    pairs = [(i, i + by) for i in range(length) if 0 <= i + by < length]
    return lax.ppermute(value, axis, pairs)


def pick_groups(product, block, per_group):
    lane = lax.broadcasted_iota(jnp.int32, (block, LANES), 1)
    total = product[:block]
    for g in range(1, LANES // per_group):
        total = jnp.where(lane >= g * per_group, product[g * block : (g + 1) * block], total)
    return total


def featurized(x, at, count, tap):
    return (
        tap[0] * x[pl.ds(at, count)] + tap[1] * x[pl.ds(at - 1, count)] + tap[2] * x[pl.ds(at - 2, count)]
    ).astype(BF16)


def spans(ref, first, count, width):
    return jnp.concatenate([ref[(first + i) * BLOCK : (first + i) * BLOCK + width] for i in range(count)], axis=1)


def kernel(
    steps, width, rows, halo, taps, per_group,
    first_ref, second_ref, values_ref, cot_ref, before_ref, after_ref, ta_ref, tb_ref, tc_ref, filters_ref, turn_ref,
    result_ref, grad_ref, fgrad_ref, sgrad_ref,
    xa, xb, xc, fa, fb, fc, mixed, gated, ahead, behind, fga, fgb, fgc, masked, held, sems,
):
    step = pl.program_id(0)
    groups = LANES // per_group
    blocks = rows // BLOCK
    span = taps + BLOCK
    reach = taps + PACK
    channels = steps * width
    row = lax.broadcasted_iota(jnp.int32, (BLOCK, taps), 0)
    col = lax.broadcasted_iota(jnp.int32, (BLOCK, taps), 1)
    zero = jnp.zeros((BLOCK, taps), F32)
    lane_group = lax.broadcasted_iota(jnp.int32, (BLOCK, LANES), 1) // per_group

    def inner(part):
        lanes = slice(part * LANES, (part + 1) * LANES)
        tap_a, tap_b, tap_c = ([ref[s : s + 1, lanes] for s in range(3)] for ref in (ta_ref, tb_ref, tc_ref))

        xa[:halo] = before_ref[:halo, lanes].astype(F32)
        xa[halo : halo + rows] = first_ref[:, lanes].astype(F32)
        xa[halo + rows :] = after_ref[2 * halo : 2 * halo + PACK, lanes].astype(F32)
        xc[:halo] = before_ref[halo : 2 * halo, lanes].astype(F32)
        xc[halo : halo + rows] = values_ref[:, lanes].astype(F32)
        xc[halo + rows :] = after_ref[2 * halo + PACK : 2 * halo + 2 * PACK, lanes].astype(F32)
        xb[:PACK] = before_ref[2 * halo : 2 * halo + PACK, lanes].astype(F32)
        xb[PACK : PACK + rows] = second_ref[:, lanes].astype(F32)
        xb[PACK + rows :] = after_ref[:halo, lanes].astype(F32)

        for r in range(0, taps + rows + PACK, PACK):
            a = featurized(xa, halo - taps + r, PACK, tap_a)
            c = featurized(xc, halo - taps + r, PACK, tap_c)
            mixed[r : r + PACK] = (a.astype(F32) * c.astype(F32)).astype(BF16)
            if r >= taps:
                fa[r - taps : r - taps + PACK] = a
                fc[r - taps : r - taps + PACK] = c
        for r in range(0, rows + halo, PACK):
            b = featurized(xb, PACK + r, PACK, tap_b)
            if r < rows:
                cot = cot_ref[r : r + PACK, lanes]
                fb[r : r + PACK] = b
            else:
                cot = after_ref[halo + r - rows : halo + r - rows + PACK, lanes]
            gated[r : r + PACK] = (b.astype(F32) * cot.astype(F32)).astype(BF16)

        straight = filters_ref[part * groups : (part + 1) * groups]
        reverse = jnp.dot(straight.astype(BF16), turn_ref[...], preferred_element_type=F32)
        for g in range(groups):
            at = slice(g * BLOCK, (g + 1) * BLOCK)
            wheel = pltpu.roll(jnp.broadcast_to(reverse[g : g + 1], (BLOCK, taps)), 0, 1, stride=1, stride_axis=0)
            ahead[at, :taps] = jnp.where(col > row, wheel, zero).astype(BF16)
            ahead[at, taps:] = jnp.where(col > row, zero, wheel).astype(BF16)
            wheel = pltpu.roll(jnp.broadcast_to(straight[g : g + 1], (BLOCK, taps)), 0, 1, stride=1, stride_axis=0)
            behind[at, :taps] = jnp.where(col >= row, wheel, zero).astype(BF16)
            behind[at, taps:] = jnp.where(col >= row, zero, wheel).astype(BF16)

        toeplitz = ahead[:, :span]
        for b in range(0, blocks, 2):
            product = jnp.dot(toeplitz, spans(mixed, b, 2, span), preferred_element_type=F32)
            for i in range(2):
                at = slice((b + i) * BLOCK, (b + i + 1) * BLOCK)
                hidden = pick_groups(product[:, i * LANES : (i + 1) * LANES], BLOCK, per_group)
                result_ref[at, lanes] = (fb[at].astype(F32) * hidden).astype(BF16)
                fgb[at] = cot_ref[at, lanes].astype(F32) * hidden
        heads = jnp.concatenate([ahead[g * BLOCK : g * BLOCK + PACK, :reach] for g in range(groups)], axis=0)
        product = jnp.dot(heads, mixed[rows : rows + reach], preferred_element_type=F32)
        fgb[rows:] = after_ref[halo : halo + PACK, lanes].astype(F32) * pick_groups(product, PACK, per_group)

        toeplitz = behind[:, :span]
        for b in range(0, blocks, 2):
            product = jnp.dot(toeplitz, spans(gated, b, 2, span), preferred_element_type=F32)
            for i in range(2):
                at = slice((b + i) * BLOCK, (b + i + 1) * BLOCK)
                grad = pick_groups(product[:, i * LANES : (i + 1) * LANES], BLOCK, per_group)
                fga[at] = grad * fc[at].astype(F32)
                fgc[at] = grad * fa[at].astype(F32)
        heads = jnp.concatenate([behind[g * BLOCK : g * BLOCK + PACK, :reach] for g in range(groups)], axis=0)
        product = jnp.dot(heads, gated[rows : rows + reach], preferred_element_type=F32)
        grad = pick_groups(product, PACK, per_group)
        fga[rows:] = grad * fc[rows:].astype(F32)
        fgc[rows:] = grad * fa[rows:].astype(F32)

        for b in range(blocks):
            block = gated[b * BLOCK : (b + 1) * BLOCK].astype(F32)
            for g in range(groups):
                masked[g * BLOCK : (g + 1) * BLOCK, b * LANES : (b + 1) * LANES] = jnp.where(
                    lane_group == g, block, 0.0
                ).astype(BF16)
        moment = lax.dot_general(
            masked[...], spans(mixed, 0, blocks, span), (((1,), (1,)), ((), ())), preferred_element_type=F32
        )
        for g in range(groups):
            at = slice(g * BLOCK, (g + 1) * BLOCK)
            later = jnp.concatenate([moment[at, taps:], jnp.zeros((BLOCK, taps - BLOCK), F32)], axis=1)
            wheel = jnp.where(col > row, moment[at, :taps], later)
            turned = wheel[:8]
            for p in range(8, BLOCK, 8):
                turned = turned + pltpu.roll(wheel[p : p + 8], taps - p, 1)
            for p in (4, 2, 1):
                turned = turned + pltpu.roll(pltpu.roll(turned, taps - p, 1), 8 - p, 0)
            fgrad_ref[part * groups + g : part * groups + g + 1] = turned[:1]

        column = pl.multiple_of(step * width + part * LANES, LANES)
        for which, (fg, x, start, tap) in enumerate(
            ((fga, xa, halo, tap_a), (fgb, xb, PACK, tap_b), (fgc, xc, halo, tap_c))
        ):
            sums = [jnp.zeros((8, LANES), F32) for _ in range(3)]
            for r in range(0, rows, PACK):
                near = [fg[pl.ds(r + s, PACK)] for s in range(3)]
                grad = tap[0] * near[0] + tap[1] * near[1] + tap[2] * near[2]
                held[r : r + PACK, pl.ds(which * channels + column, LANES)] = grad.astype(BF16)
                own = x[start + r : start + r + PACK]
                for s in range(3):
                    term = near[s] * own
                    sums[s] = sums[s] + (term[:8] + term[8:])
            for s in range(3):
                sgrad_ref[which, s : s + 1, lanes] = jnp.sum(sums[s], axis=0, keepdims=True)

    for part in range(width // LANES):
        inner(part)

    def copy(at, which):
        columns = pl.ds(pl.multiple_of(which * channels + at * width, LANES), width)
        return pltpu.make_async_copy(held.at[:, columns], grad_ref.at[:, columns], sems.at[which])

    for which in range(3):
        copy(step, which).start()

    @pl.when(step == steps - 1)
    def _():
        for which in range(3):
            columns = pl.ds(which * channels, channels)
            pltpu.make_async_copy(held.at[:, columns], grad_ref.at[:, columns], sems.at[which]).wait()


def local(stream, cot, before, after, filters, tap_rows, halo, width=2 * LANES):
    rows, channels = cot.shape
    group_count, taps = filters.shape
    per_group = channels // group_count
    steps = channels // width
    groups = width // per_group
    span = taps + BLOCK
    index = np.arange(taps)
    turn = jnp.asarray(index[:, None] == (-index[None, :]) % taps, BF16)

    def column(offset, height):
        return pl.BlockSpec((height, width), lambda j: (0, offset * steps + j))

    return pl.pallas_call(
        functools.partial(kernel, steps, width, rows, halo, taps, per_group),
        grid=(steps,),
        in_specs=[column(w, rows) for w in range(3)]
        + [column(0, rows), column(0, before.shape[0]), column(0, after.shape[0])]
        + [column(w, 3) for w in range(3)]
        + [pl.BlockSpec((groups, taps), lambda j: (j, 0)), pl.BlockSpec((taps, taps), lambda j: (0, 0))],
        out_specs=[
            column(0, rows),
            pl.BlockSpec(memory_space=pl.ANY),
            pl.BlockSpec((groups, taps), lambda j: (j, 0)),
            pl.BlockSpec((3, 3, width), lambda j: (0, 0, j)),
        ],
        out_shape=[
            jax.ShapeDtypeStruct((rows, channels), BF16),
            jax.ShapeDtypeStruct((rows, 3 * channels), BF16),
            jax.ShapeDtypeStruct((group_count, taps), F32),
            jax.ShapeDtypeStruct((3, 3, channels), F32),
        ],
        scratch_shapes=[
            pltpu.VMEM((halo + rows + PACK, LANES), F32),
            pltpu.VMEM((PACK + rows + halo, LANES), F32),
            pltpu.VMEM((halo + rows + PACK, LANES), F32),
            pltpu.VMEM((rows + PACK, LANES), BF16),
            pltpu.VMEM((rows, LANES), BF16),
            pltpu.VMEM((rows + PACK, LANES), BF16),
            pltpu.VMEM((taps + rows + PACK, LANES), BF16),
            pltpu.VMEM((rows + halo, LANES), BF16),
            pltpu.VMEM((LANES // per_group * BLOCK, 2 * taps), BF16),
            pltpu.VMEM((LANES // per_group * BLOCK, 2 * taps), BF16),
            pltpu.VMEM((rows + PACK, LANES), F32),
            pltpu.VMEM((rows + PACK, LANES), F32),
            pltpu.VMEM((rows + PACK, LANES), F32),
            pltpu.VMEM((LANES // per_group * BLOCK, rows // BLOCK * LANES), BF16),
            pltpu.VMEM((rows, 3 * channels), BF16),
            pltpu.SemaphoreType.DMA((3,)),
        ],
        compiler_params=pltpu.CompilerParams(vmem_limit_bytes=48 * 1024 * 1024),
        name="hyena_block",
    )(stream, stream, stream, cot, before, after, tap_rows, tap_rows, tap_rows, filters, turn)


def on_device(streams, cotangent, filters, short_taps):
    stream, cot = streams[0], cotangent[0]
    rows, channels = cot.shape
    own_groups, taps = filters.shape
    own_taps = short_taps.shape[1]
    device_count = lax.axis_size("fsdp") * lax.axis_size("ctx")
    group_count = own_groups * device_count
    halo = taps + PACK
    first, second, values = (stream[:, w * channels : (w + 1) * channels] for w in range(3))

    before = shifted(
        jnp.concatenate([first[rows - halo :], values[rows - halo :], second[rows - PACK :]], axis=0), "ctx", 1
    )
    after = shifted(jnp.concatenate([second[:halo], cot[:halo], first[:PACK], values[:PACK]], axis=0), "ctx", -1)

    padding = -own_taps % LANES
    own = jnp.concatenate(
        [filters.reshape(1, -1), jnp.pad(short_taps, ((0, 0), (0, padding))).reshape(1, -1)], axis=1
    )
    whole = lax.all_to_all(
        jnp.broadcast_to(own, (device_count, own.shape[1])), ("fsdp", "ctx"), 0, 0, tiled=True
    )
    whole_filters = whole[:, : own_groups * taps].reshape(group_count, taps)
    whole_taps = whole[:, own_groups * taps :].reshape(device_count, 3, own_taps + padding)[:, :, :own_taps]
    whole_taps = whole_taps.transpose(1, 0, 2).reshape(3, device_count * own_taps)

    result, stream_grad, filter_part, short_part = local(stream, cot, before, after, whole_filters, whole_taps, halo)

    filter_part = filter_part.reshape(device_count, own_groups * taps)
    short_part = short_part.transpose(1, 0, 2).reshape(3, device_count, own_taps).transpose(1, 0, 2)
    short_part = jnp.pad(short_part, ((0, 0), (0, 0), (0, padding))).reshape(device_count, -1)
    terms = lax.all_to_all(
        jnp.concatenate([filter_part, short_part], axis=1), ("fsdp", "ctx"), 0, 0, tiled=True
    )
    factor = 1.0 / math.sqrt(device_count * rows)
    total = jnp.sum(terms, axis=0) * factor
    filter_grad = jnp.roll(total[: own_groups * taps].reshape(own_groups, taps)[:, ::-1], 1, axis=1)
    short_grad = total[own_groups * taps :].reshape(3, own_taps + padding)[:, :own_taps]
    return (result[None], stream_grad[None], filter_grad, short_grad)


def solution(mesh):
    in_specs = (
        P("fsdp", "ctx", None),
        P("fsdp", "ctx", None),
        P(("fsdp", "ctx"), None),
        P(None, ("fsdp", "ctx")),
    )
    out_specs = (
        P("fsdp", "ctx", None),
        P("fsdp", "ctx", None),
        P(("fsdp", "ctx"), None),
        P(None, ("fsdp", "ctx")),
    )
    return jax.shard_map(
        on_device, mesh=mesh, in_specs=in_specs, out_specs=out_specs, check_vma=False
    )
```

time: 1910 us -> 119 us (0.06)
  waiting for transfers between devices: 705 us -> 0.01 us
  local copies, waits for them, and re-layouts: 683 us -> 6.13 us
  blocking collectives: 352 us -> 60.3 us
  other arithmetic: 97 us -> 4.29 us
  Pallas kernels: 0 us -> 40.5 us
  matrix products: 33.8 us -> 0 us
    unnamed x4 -> x0, waiting for transfers between devices: 705 us -> none
    gather x5 -> x0, local copies, waits for them, and re-layouts: 565 us -> none  [the longest x4 305 us: build_kernels(): picked = narrow[:, np.clip(lag_table, 0, tap_count - 1)]]
    all_gather x2 -> x0, blocking collectives: 352 us -> none  [the longest x1 178 us: on_device(): lax.all_gather(short_taps, ('fsdp', 'ctx'), axis=1, tiled=True)]
    all_to_all x0 -> x2, blocking collectives: none -> 60.3 us  [the longest x1 42.1 us: on_device(): lax.all_to_all(jnp.broadcast_to(own, (device_count, own.shape[1])), ('fsd...]
    dot_general x3 -> x0, local copies, waits for them, and re-layouts: 41.6 us -> none  [the longest x1 35 us: on_device(): jnp.einsum('gcbi,gcbj->gij', gate_blocks, mixed_blocks, preferred_element...]
    pallas_call x0 -> x1, Pallas kernels: none -> 40.5 us  [local(): pl.pallas_call(functools.partial(kernel, steps, width, rows, halo, taps,...]
    reduce_sum x2 -> x1, other arithmetic: 38.3 us -> 0.25 us  [on_device(): total = jnp.sum(terms, axis=0) * factor]
    unnamed x67 -> x11, local copies, waits for them, and re-layouts: 36.3 us -> 0.31 us
  transfers between devices with their start and end apart: 6 -> 2, of which waited for: 2 -> 0; matrix products, arithmetic and copies ran while one was open for 36% -> 2% of each run, Pallas kernels for 0% -> 0%
where the time goes in v1:
time: 119 us
  blocking collectives  60.3 us (51%)
  Pallas kernels  40.5 us (34%)
  starting transfers between devices  6.76 us (6%)
  local copies, waits for them, and re-layouts  6.13 us (5%)
  other arithmetic  4.29 us (4%)
    all_to_all x1, blocking collectives, on_device(): lax.all_to_all(jnp.broadcast_to(own, (device_count, own.shape[1])), ('fsd...  42.1 us
    pallas_call x1, Pallas kernels, local(): pl.pallas_call(functools.partial(kernel, steps, width, rows, halo, taps,...  40.5 us
    all_to_all x1, blocking collectives, on_device(): lax.all_to_all(jnp.concatenate([filter_part, short_part], axis=1), ('fsdp...  18.2 us
    ppermute x2, starting transfers between devices, shifted(): return lax.ppermute(value, axis, pairs)  6.76 us
    slice x1, local copies, waits for them, and re-layouts, on_device(): second[:halo]  2.47 us
  transfers between devices with their start and end apart: 2, of which 0 were waited for; matrix products, arithmetic and copies ran while one was open for 2% of the time, Pallas kernels for 0%

profile of v1, /device:TPU:1, one launch (start us, length us, event | category | flops | bytes accessed | tf_op | source)
XLA Modules:
  0.0 118.8 jit_solution(3816011046645409744)
XLA Ops:
  0.6 1.1 fusion.1
  1.7 0.0 copy-start
  1.7 2.5 %fusion = (bf16[144,4096]{1,0:T(8,128)(2,1)S(1)}, bf16[144,4096]{1,0:T(8,128)(2,1)S(1)}, bf16[144,4096]{1,0:T(8,128)(2,1)S(1)}) fusion(bf16[256,12288]{1,0:T(8,128)(2,1)} %bitcast.27), kind=kLoop, calls=%fused_computation.10 | loop fusion | bytes 7077888 | tf_op jit(solution)/shard_map/slice | solution.py:247
  4.2 0.2 copy-done
  4.4 0.1 slice_bitcast_fusion
  4.5 1.6 %pad_maximum_fusion = bf16[320,4096]{1,0:T(8,128)(2,1)} fusion(bf16[16,4096]{1,0:T(8,128)(2,1)S(1)} %get-tuple-element.16, bf16[16,4096]{1,0:T(8,128)(2,1)S(1)} %get-tuple-element.15, bf16[144,4096]{1,0:T(8,128)(2,1)S(1)} %slice_bitcast_fusion, bf16[144,4096]{1,0:T(8,128)(2,1)S(1)} %get-tuple-element.12), kind=kLoop, calls=%fused_computation | loop fusion | flops 10485760 | bytes 5242880 | tf_op jit(solution)/shard_map/concatenate | solution.py:247
  6.1 3.5 %collective-permute-start.1 = (bf16[320,4096]{1,0:T(8,128)(2,1)}, bf16[320,4096]{1,0:T(8,128)(2,1)}, u32[]{:S(2)}, u32[]{:S(2)}) collective-permute-start(bf16[320,4096]{1,0:T(8,128)(2,1)} %pad_maximum_fusion), channel_id=1, source_target_pairs={{1,0},{2,1},{3,2},{4,3},{5,4},{6,5},{7,6},{8,7},{9,8},{10,9},{11,1... | collective-permute-start | bytes 7864328 | tf_op jit(solution)/shard_map/ppermute | solution.py:21
  9.5 1.8 %pad_maximum_fusion.1 = bf16[304,4096]{1,0:T(8,128)(2,1)} fusion(bf16[16,4096]{1,0:T(8,128)(2,1)S(1)} %get-tuple-element.17, bf16[144,4096]{1,0:T(8,128)(2,1)S(1)} %get-tuple-element.13, bf16[144,4096]{1,0:T(8,128)(2,1)S(1)} %get-tuple-element.14), kind=kLoop, calls=%fused_computation.1 | loop fusion | flops 7471104 | bytes 4980736 | tf_op jit(solution)/shard_map/concatenate | solution.py:245
  11.3 3.3 %collective-permute-start = (bf16[304,4096]{1,0:T(8,128)(2,1)}, bf16[304,4096]{1,0:T(8,128)(2,1)}, u32[]{:S(2)}, u32[]{:S(2)}) collective-permute-start(bf16[304,4096]{1,0:T(8,128)(2,1)} %pad_maximum_fusion.1), channel_id=1, source_target_pairs={{0,1},{1,2},{2,3},{3,4},{4,5},{5,6},{6,7},{7,8},{8,9},{9,10},{10,1... | collective-permute-start | bytes 7471112 | tf_op jit(solution)/shard_map/ppermute | solution.py:21
  14.6 0.0 copy-done.2
  14.6 0.0 copy-done.3
  14.7 0.2 broadcast_in_dim.11
  14.8 42.1 %all_to_all.18 = f32[128,1,640]{2,1,0:T(1,128)S(1)} all-to-all(f32[128,1,640]{2,1,0:T(1,128)S(1)} %broadcast_in_dim.11), channel_id=1, replica_groups=mesh['fsdp'=8,'ctx'=16] {'fsdp','ctx'}, dimensions={0} | all-to-all | bytes 655360 | tf_op jit(solution)/shard_map/all_to_all | solution.py:253
  56.9 0.2 copy.15
  57.1 0.1 copy.17
  57.3 0.1 copy.16
  57.4 0.2 reshape.52.ta_ref.tb_ref.tc_ref
  57.6 0.0 collective-permute-done.before_ref
  57.6 0.0 collective-permute-done.1.after_ref
  57.6 0.0 copy-done.1
  57.6 40.5 %hyena_block.1 = (bf16[256,4096]{1,0:T(8,128)(2,1)}, bf16[256,12288]{1,0:T(8,128)(2,1)}, f32[256,128]{1,0:T(8,128)S(1)}, f32[3,3,4096]{2,1,0:T(4,128)S(1)}) custom-call(bf16[256,12288]{1,0:T(8,128)(2,1)} %bitcast.28, bf16[256,12288]{1,0:T(8,128)(2,1)} %bitcast.29, bf16[256,12288]{1,0:T(8,128)(2,1)} %bitcast.30, bf16[256,4096]{1,0:T(8,128)(2,1)S(1)} %bitcast.24, ...), custom_call_target="tpu_custom_call" | custom-call | tf_op jit(solution)/shard_map/hyena_block/pallas_call | solution.py:192
  98.2 0.1 copy.20
  98.3 0.1 copy.18
  98.4 0.2 reshape.55
  98.5 0.1 copy.22
  98.7 0.2 copy.21
  98.9 18.2 %all_to_all.19 = f32[128,1,640]{2,1,0:T(1,128)S(1)} all-to-all(f32[128,1,640]{2,1,0:T(1,128)S(1)} %copy.21), channel_id=1, replica_groups=mesh['fsdp'=8,'ctx'=16] {'fsdp','ctx'}, dimensions={0} | all-to-all | bytes 655360 | tf_op jit(solution)/shard_map/all_to_all | solution.py:265
  117.2 0.2 reduce_sum.9
  117.4 0.1 slice.76
  117.5 0.6 slice.78
  118.1 0.1 slice.77
  118.2 0.6 pad_maximum_fusion.2
  (15 shorter events, 0.2 us)
Async XLA Ops:
  1.7 2.7 %copy-start = (bf16[1,256,4096]{2,1,0:T(8,128)(2,1)S(1)}, bf16[1,256,4096]{2,1,0:T(8,128)(2,1)}, u32[]{:S(2)}) copy-start(bf16[1,256,4096]{2,1,0:T(8,128)(2,1)} %param.6) | copy-start | bytes 6291460
  6.1 8.5 %copy-start.2 = (f32[3,96]{1,0:T(4,128)S(1)}, f32[3,96]{1,0:T(4,128)}, u32[]{:S(2)}) copy-start(f32[3,96]{1,0:T(4,128)} %param.8) | copy-start | bytes 3460
  6.1 8.6 %copy-start.3 = (f32[2,128]{1,0:T(2,128)S(1)}, f32[2,128]{1,0:T(2,128)}, u32[]{:S(2)}) copy-start(f32[2,128]{1,0:T(2,128)} %param.7) | copy-start | bytes 3076
  6.1 51.6 %collective-permute-start.1 = (bf16[320,4096]{1,0:T(8,128)(2,1)}, bf16[320,4096]{1,0:T(8,128)(2,1)}, u32[]{:S(2)}, u32[]{:S(2)}) collective-permute-start(bf16[320,4096]{1,0:T(8,128)(2,1)} %pad_maximum_fusion), channel_id=1, source_target_pairs={{1,0},{2,1},{3,2},{4,3},{5,4},{6,5},{7,6},{8,7},{9,8},{10,9},{11,1... | collective-permute-start | bytes 7864328 | tf_op jit(solution)/shard_map/ppermute | solution.py:21
  11.3 46.4 %copy-start.1 = (bf16[128,128]{1,0:T(8,128)(2,1)S(1)}, bf16[128,128]{1,0:T(8,128)(2,1)}, u32[]{:S(2)}) copy-start(bf16[128,128]{1,0:T(8,128)(2,1)} %constant.8.clone.turn_ref) | copy-start | bytes 98308
  11.3 46.3 %collective-permute-start = (bf16[304,4096]{1,0:T(8,128)(2,1)}, bf16[304,4096]{1,0:T(8,128)(2,1)}, u32[]{:S(2)}, u32[]{:S(2)}) collective-permute-start(bf16[304,4096]{1,0:T(8,128)(2,1)} %pad_maximum_fusion.1), channel_id=1, source_target_pairs={{0,1},{1,2},{2,3},{3,4},{4,5},{5,6},{6,7},{7,8},{8,9},{9,10},{10,1... | collective-permute-start | bytes 7471112 | tf_op jit(solution)/shard_map/ppermute | solution.py:21

commit v2 on v1

v2 whole, which is shorter than its diff:
```python
import functools
import math

import jax
import jax.numpy as jnp
import numpy as np
from jax import lax
from jax.experimental import pallas as pl
from jax.experimental.pallas import tpu as pltpu
from jax.sharding import PartitionSpec as P

F32, BF16 = jnp.float32, jnp.bfloat16
LANES = 128
PACK = 16
BLOCK = 32
PITCH = BLOCK + 8
LEAD = 8
PARTS = 1
VMEM = 56 * 1024 * 1024


def shifted(value, axis, by):
    length = lax.axis_size(axis)
    pairs = [(i, i + by) for i in range(length) if 0 <= i + by < length]
    return lax.ppermute(value, axis, pairs)


def pick_groups(product, block, per_group):
    lane = lax.broadcasted_iota(jnp.int32, (block, LANES), 1)
    total = product[:block]
    for g in range(1, LANES // per_group):
        total = jnp.where(lane >= g * per_group, product[g * block : (g + 1) * block], total)
    return total


def featurized(x, at, count, tap):
    return (
        tap[0] * x[pl.ds(at, count)] + tap[1] * x[pl.ds(at - 1, count)] + tap[2] * x[pl.ds(at - 2, count)]
    ).astype(BF16)


def spans(ref, first, count, width):
    return jnp.concatenate([ref[(first + i) * BLOCK : (first + i) * BLOCK + width] for i in range(count)], axis=1)


def taps_of(refs, lanes):
    return [[ref[s : s + 1, lanes] for s in range(3)] for ref in refs]


def toeplitz_kernel(taps, filters_ref, turn_ref, ahead_ref, behind_ref):
    row = lax.broadcasted_iota(jnp.int32, (BLOCK, taps), 0)
    col = lax.broadcasted_iota(jnp.int32, (BLOCK, taps), 1)
    zero = jnp.zeros((BLOCK, taps), F32)
    straight = filters_ref[...]
    reverse = jnp.dot(straight.astype(BF16), turn_ref[...], preferred_element_type=F32)
    for g in range(straight.shape[0]):
        at = slice(g * BLOCK, (g + 1) * BLOCK)
        wheel = pltpu.roll(jnp.broadcast_to(reverse[g : g + 1], (BLOCK, taps)), 0, 1, stride=1, stride_axis=0)
        ahead_ref[at, :taps] = jnp.where(col > row, wheel, zero).astype(BF16)
        ahead_ref[at, taps:] = jnp.where(col > row, zero, wheel).astype(BF16)
        wheel = pltpu.roll(jnp.broadcast_to(straight[g : g + 1], (BLOCK, taps)), 0, 1, stride=1, stride_axis=0)
        behind_ref[at, :taps] = jnp.where(col >= row, wheel, zero).astype(BF16)
        behind_ref[at, taps:] = jnp.where(col >= row, zero, wheel).astype(BF16)


def toeplitz_blocks(filters, batch=64):
    group_count, taps = filters.shape
    index = np.arange(taps)
    turn = jnp.asarray(index[:, None] == (-index[None, :]) % taps, BF16)
    out = pl.BlockSpec((batch * BLOCK, 2 * taps), lambda j: (j, 0))
    shape = jax.ShapeDtypeStruct((group_count * BLOCK, 2 * taps), BF16)
    return pl.pallas_call(
        functools.partial(toeplitz_kernel, taps),
        grid=(group_count // batch,),
        in_specs=[pl.BlockSpec((batch, taps), lambda j: (j, 0)), pl.BlockSpec((taps, taps), lambda j: (0, 0))],
        out_specs=[out, out],
        out_shape=[shape, shape],
        compiler_params=pltpu.CompilerParams(vmem_limit_bytes=VMEM),
        cost_estimate=pl.CostEstimate(flops=10**9, bytes_accessed=10**7, transcendentals=0),
        name="toeplitz_blocks",
    )(filters, turn)


def edge_kernel(
    width, taps,
    first_lead, first_tail, values_lead, values_tail, first_head, values_head, second_head, second_next,
    cot_head, cot_next, tail_a, tail_b, tail_c, ta_ref, tb_ref, tc_ref,
    mixed_ref, gated_ref,
    xa, xb, xc, xs, xt, tile,
):
    for part in range(width // LANES):
        lanes = slice(part * LANES, (part + 1) * LANES)
        tap_a, tap_b, tap_c = taps_of((ta_ref, tb_ref, tc_ref), lanes)
        for x, lead, tail in ((xa, first_lead, first_tail), (xc, values_lead, values_tail)):
            x[:PACK] = lead[:, lanes].astype(F32)
            x[PACK:] = tail[:, lanes].astype(F32)
        for r in range(0, taps, PACK):
            a = featurized(xa, PACK + r, PACK, tap_a)
            c = featurized(xc, PACK + r, PACK, tap_c)
            mixed_ref[r : r + PACK, lanes] = (a.astype(F32) * c.astype(F32)).astype(BF16)
        xb[:LEAD] = tail_b[:, lanes]
        xb[LEAD : LEAD + taps] = second_head[:, lanes].astype(F32)
        xb[LEAD + taps :] = second_next[:, lanes].astype(F32)
        for r in range(0, taps, PACK):
            b = featurized(xb, LEAD + r, PACK, tap_b)
            gated_ref[r : r + PACK, lanes] = (b.astype(F32) * cot_head[r : r + PACK, lanes].astype(F32)).astype(BF16)
        b = featurized(xb, LEAD + taps, PACK, tap_b)
        for x, lead, head in ((xs, tail_a, first_head), (xt, tail_c, values_head)):
            x[:LEAD] = lead[:, lanes]
            x[LEAD:] = head[:, lanes].astype(F32)
        tile[...] = jnp.zeros_like(tile)
        tile[:1] = (b.astype(F32) * cot_next[:, lanes].astype(F32))[:1]
        tile[1:3] = featurized(xs, LEAD, PACK, tap_a).astype(F32)[:2]
        tile[3:5] = featurized(xt, LEAD, PACK, tap_c).astype(F32)[:2]
        tile[5:7] = cot_head[:PACK, lanes].astype(F32)[:2]
        gated_ref[taps:, lanes] = tile[...].astype(BF16)


def edges(part, stream, cot, tails, tap_rows, taps, width=8 * LANES):
    rows, channels = cot.shape
    all_steps = channels // width
    steps = all_steps // PARTS

    def column(which, height, at=0):
        return pl.BlockSpec((height, width), lambda j: (at, which * all_steps + part * steps + j))

    lead, last = (rows - taps) // PACK - 1, rows // taps - 1
    own = lambda j: (0, j)
    return pl.pallas_call(
        functools.partial(edge_kernel, width, taps),
        grid=(steps,),
        in_specs=[column(0, PACK, lead), column(0, taps, last), column(2, PACK, lead), column(2, taps, last)]
        + [column(0, PACK), column(2, PACK), column(1, taps), column(1, PACK, taps // PACK)]
        + [column(0, taps), column(0, PACK, taps // PACK)]
        + [column(w, LEAD) for w in range(3)]
        + [column(w, 3) for w in range(3)],
        out_specs=[pl.BlockSpec((taps, width), own), pl.BlockSpec((taps + PACK, width), own)],
        out_shape=[
            jax.ShapeDtypeStruct((taps, steps * width), BF16),
            jax.ShapeDtypeStruct((taps + PACK, steps * width), BF16),
        ],
        scratch_shapes=[
            pltpu.VMEM((PACK + taps, LANES), F32),
            pltpu.VMEM((LEAD + taps + PACK, LANES), F32),
            pltpu.VMEM((PACK + taps, LANES), F32),
            pltpu.VMEM((LEAD + PACK, LANES), F32),
            pltpu.VMEM((LEAD + PACK, LANES), F32),
            pltpu.VMEM((PACK, LANES), F32),
        ],
        compiler_params=pltpu.CompilerParams(vmem_limit_bytes=VMEM),
        cost_estimate=pl.CostEstimate(flops=10**7, bytes_accessed=4 * 10**6, transcendentals=0),
        name="edges",
    )(*[stream] * 8, cot, cot, *[tails] * 3, *[tap_rows] * 3)


def main_kernel(
    part, steps, width, rows, channels, taps, per_group, aliased, *refs
):
    (first_ref, second_ref, values_ref, cot_ref, before_ref, after_ref, tail_a, tail_b, tail_c,
     ta_ref, tb_ref, tc_ref, ahead, behind) = refs[:14]
    result_ref, grad_ref, fgrad_ref, sgrad_ref = refs[14 + aliased : 18 + aliased]
    *buffers, wheels, held, sems = refs[18 + aliased :]
    step = pl.program_id(0)
    groups = LANES // per_group
    blocks = rows // BLOCK
    span = taps + BLOCK
    reach = taps + PACK
    inner_parts = width // LANES
    row = lax.broadcasted_iota(jnp.int32, (BLOCK, taps), 0)
    col = lax.broadcasted_iota(jnp.int32, (BLOCK, taps), 1)
    lane = lax.broadcasted_iota(jnp.int32, (BLOCK, LANES), 1)

    def diagonal_sums(at):
        for p in range(inner_parts):
            total = jnp.zeros((groups, taps), F32)
            for i in range(BLOCK):
                turned = wheels[pl.ds(p * groups * PITCH + i, groups, stride=PITCH), :]
                total = total + (pltpu.roll(turned, taps - i, 1) if i else turned)
            fgrad_ref[pl.ds(pl.multiple_of((at * inner_parts + p) * groups, groups), groups), :] = total

    diagonal_sums(jnp.maximum(step - 1, 0))

    def inner(p):
        lanes = slice(p * LANES, (p + 1) * LANES)
        xa, xb, xc, fa, fb, fc, mixed, gated, fga, fgb, fgc, masked, tile = (ref.at[p] for ref in buffers)
        tap_a, tap_b, tap_c = taps_of((ta_ref, tb_ref, tc_ref), lanes)
        for x, lead, own in ((xa, tail_a, first_ref), (xb, tail_b, second_ref), (xc, tail_c, values_ref)):
            x[:LEAD] = lead[:, lanes]
            x[LEAD:] = own[:, lanes].astype(F32)
        tile[:PACK] = after_ref[taps:, lanes].astype(F32)
        tile[PACK:] = jnp.zeros((PACK, LANES), F32)

        mixed[:taps] = before_ref[:, lanes]
        for r in range(0, rows, PACK):
            a = featurized(xa, LEAD + r, PACK, tap_a)
            c = featurized(xc, LEAD + r, PACK, tap_c)
            mixed[taps + r : taps + r + PACK] = (a.astype(F32) * c.astype(F32)).astype(BF16)
            fa[r : r + PACK] = a
            fc[r : r + PACK] = c
        mixed[taps + rows :] = (tile[1 : 1 + PACK] * tile[3 : 3 + PACK]).astype(BF16)
        for r in range(0, rows, PACK):
            b = featurized(xb, LEAD + r, PACK, tap_b)
            fb[r : r + PACK] = b
            gated[r : r + PACK] = (b.astype(F32) * cot_ref[r : r + PACK, lanes].astype(F32)).astype(BF16)
        gated[rows : rows + taps] = after_ref[:taps, lanes]
        gated[rows + taps :] = jnp.where(row[:PACK] == 0, tile[:PACK], 0.0).astype(BF16)

        top = p * groups * BLOCK

        toeplitz = ahead[top : top + groups * BLOCK, :span]
        for b in range(0, blocks, 2):
            product = jnp.dot(toeplitz, spans(mixed, b, 2, span), preferred_element_type=F32)
            for i in range(2):
                at = slice((b + i) * BLOCK, (b + i + 1) * BLOCK)
                hidden = pick_groups(product[:, i * LANES : (i + 1) * LANES], BLOCK, per_group)
                result_ref[at, lanes] = (fb[at].astype(F32) * hidden).astype(BF16)
                fgb[at] = cot_ref[at, lanes].astype(F32) * hidden
        heads = [slice(top + g * BLOCK, top + g * BLOCK + PACK) for g in range(groups)]
        product = jnp.dot(
            jnp.concatenate([ahead[at, :reach] for at in heads], axis=0),
            mixed[rows : rows + reach],
            preferred_element_type=F32,
        )
        fgb[rows:] = tile[5 : 5 + PACK] * pick_groups(product, PACK, per_group)

        toeplitz = behind[top : top + groups * BLOCK, :span]
        for b in range(0, blocks, 2):
            product = jnp.dot(toeplitz, spans(gated, b, 2, span), preferred_element_type=F32)
            for i in range(2):
                at = slice((b + i) * BLOCK, (b + i + 1) * BLOCK)
                grad = pick_groups(product[:, i * LANES : (i + 1) * LANES], BLOCK, per_group)
                fga[at] = grad * fc[at].astype(F32)
                fgc[at] = grad * fa[at].astype(F32)
        product = jnp.dot(
            jnp.concatenate([behind[at, :reach] for at in heads], axis=0),
            gated[rows : rows + reach],
            preferred_element_type=F32,
        )
        grad = pick_groups(product, PACK, per_group)
        fga[rows:] = grad * tile[3 : 3 + PACK]
        fgc[rows:] = grad * tile[1 : 1 + PACK]

        for b in range(blocks):
            block = gated[b * BLOCK : (b + 1) * BLOCK].astype(F32)
            for g in range(groups):
                here = (lane >= g * per_group) & (lane < (g + 1) * per_group)
                masked[g * BLOCK : (g + 1) * BLOCK, b * LANES : (b + 1) * LANES] = jnp.where(here, block, 0.0).astype(
                    BF16
                )
        moment = lax.dot_general(
            masked[...], spans(mixed, 0, blocks, span), (((1,), (1,)), ((), ())), preferred_element_type=F32
        )
        for g in range(groups):
            at = slice(g * BLOCK, (g + 1) * BLOCK)
            later = jnp.concatenate([moment[at, taps:], jnp.zeros((BLOCK, taps - BLOCK), F32)], axis=1)
            start = (p * groups + g) * PITCH
            wheels[start : start + BLOCK] = jnp.where(col > row, moment[at, :taps], later)

        column = pl.multiple_of(step * width + p * LANES, LANES)
        for which, (fg, x, tap) in enumerate(((fga, xa, tap_a), (fgb, xb, tap_b), (fgc, xc, tap_c))):
            sums = [jnp.zeros((8, LANES), F32) for _ in range(3)]
            for r in range(0, rows, PACK):
                near = [fg[pl.ds(r + s, PACK)] for s in range(3)]
                grad = tap[0] * near[0] + tap[1] * near[1] + tap[2] * near[2]
                held[r : r + PACK, pl.ds(which * steps * width + column, LANES)] = grad.astype(BF16)
                own = x[LEAD + r : LEAD + r + PACK]
                for s in range(3):
                    term = near[s] * own
                    sums[s] = sums[s] + (term[:8] + term[8:])
            for s in range(3):
                sgrad_ref[which, s : s + 1, lanes] = jnp.sum(sums[s], axis=0, keepdims=True)

    for p in range(inner_parts):
        inner(p)

    def copy(which, first, count):
        source = pl.ds(pl.multiple_of(which * steps * width + first, LANES), count)
        target = pl.ds(pl.multiple_of(which * channels + part * steps * width + first, LANES), count)
        return pltpu.make_async_copy(held.at[:, source], grad_ref.at[:, target], sems.at[which])

    for which in range(3):
        copy(which, step * width, width).start()

    @pl.when(step == steps - 1)
    def _():
        diagonal_sums(step)
        for which in range(3):
            copy(which, 0, steps * width).wait()


def main(part, stream, cot, before, after, tails, tap_rows, ahead, behind, earlier, taps, per_group, width=2 * LANES):
    rows, channels = cot.shape
    all_steps = channels // width
    steps = all_steps // PARTS
    groups = width // per_group
    offset = part * steps

    def column(which, height):
        return pl.BlockSpec((height, width), lambda j: (0, which * all_steps + offset + j))

    def own(height):
        return pl.BlockSpec((height, width), lambda j: (0, j))

    table = pl.BlockSpec((groups * BLOCK, 2 * taps), lambda j: (offset + j, 0))
    stacked = LANES // per_group * BLOCK
    inner = width // LANES
    outs = [jax.ShapeDtypeStruct((rows, channels), BF16), jax.ShapeDtypeStruct((rows, 3 * channels), BF16)]
    return pl.pallas_call(
        functools.partial(main_kernel, part, steps, width, rows, channels, taps, per_group, len(earlier)),
        grid=(steps,),
        in_specs=[column(w, rows) for w in range(3)]
        + [column(0, rows), own(taps), own(taps + PACK)]
        + [column(w, LEAD) for w in range(3)]
        + [column(w, 3) for w in range(3)]
        + [table, table]
        + [pl.BlockSpec(memory_space=pl.ANY)] * len(earlier),
        out_specs=[
            column(0, rows),
            pl.BlockSpec(memory_space=pl.ANY),
            pl.BlockSpec((steps * groups, taps), lambda j: (0, 0)),
            pl.BlockSpec((3, 3, width), lambda j: (0, 0, j)),
        ],
        out_shape=outs
        + [
            jax.ShapeDtypeStruct((steps * groups, taps), F32),
            jax.ShapeDtypeStruct((3, 3, steps * width), F32),
        ],
        scratch_shapes=[pltpu.VMEM((inner, LEAD + rows, LANES), F32)] * 3
        + [pltpu.VMEM((inner, rows, LANES), BF16)] * 3
        + [pltpu.VMEM((inner, taps + rows + PACK, LANES), BF16)] * 2
        + [pltpu.VMEM((inner, rows + PACK, LANES), F32)] * 3
        + [
            pltpu.VMEM((inner, stacked, rows // BLOCK * LANES), BF16),
            pltpu.VMEM((inner, 2 * PACK, LANES), F32),
            pltpu.VMEM((width // per_group * PITCH, taps), F32),
            pltpu.VMEM((rows, 3 * steps * width), BF16),
            pltpu.SemaphoreType.DMA((3,)),
        ],
        input_output_aliases={14 + i: i for i in range(len(earlier))},
        compiler_params=pltpu.CompilerParams(vmem_limit_bytes=VMEM),
        cost_estimate=pl.CostEstimate(flops=10**10, bytes_accessed=2 * 10**7, transcendentals=0),
        name="hyena_main",
    )(*[stream] * 3, cot, before, after, *[tails] * 3, *[tap_rows] * 3, ahead, behind, *earlier)


def on_device(streams, cotangent, filters, short_taps):
    stream, cot = streams[0], cotangent[0]
    rows, channels = cot.shape
    own_groups, taps = filters.shape
    own_taps = short_taps.shape[1]
    device_count = lax.axis_size("fsdp") * lax.axis_size("ctx")
    group_count = own_groups * device_count
    per_group = channels // group_count

    tails = shifted(stream[rows - 2 :], "ctx", 1)
    tails = jnp.pad(tails.astype(F32), ((LEAD - 2, 0), (0, 0)))

    padding = -own_taps % LANES
    own = jnp.concatenate(
        [filters.reshape(1, -1), jnp.pad(short_taps, ((0, 0), (0, padding))).reshape(1, -1)], axis=1
    )
    whole = lax.all_to_all(
        jnp.broadcast_to(own, (device_count, own.shape[1])), ("fsdp", "ctx"), 0, 0, tiled=True
    )
    whole_filters = whole[:, : own_groups * taps].reshape(group_count, taps)
    whole_taps = whole[:, own_groups * taps :].reshape(device_count, 3, own_taps + padding)[:, :, :own_taps]
    whole_taps = whole_taps.transpose(1, 0, 2).reshape(3, device_count * own_taps)

    halos = []
    for part in range(PARTS):
        mixed_tail, gated_head = edges(part, stream, cot, tails, whole_taps, taps)
        halos.append((shifted(mixed_tail, "ctx", 1), shifted(gated_head, "ctx", -1)))
    ahead, behind = toeplitz_blocks(whole_filters)
    earlier, filter_parts, short_parts = (), [], []
    for part in range(PARTS):
        result, stream_grad, filter_part, short_part = main(
            part, stream, cot, *halos[part], tails, whole_taps, ahead, behind, earlier, taps, per_group
        )
        earlier = (result, stream_grad)
        filter_parts.append(filter_part)
        short_parts.append(short_part)

    filter_part = jnp.concatenate(filter_parts, axis=0).reshape(device_count, own_groups * taps)
    short_part = jnp.concatenate(short_parts, axis=2)
    short_part = short_part.transpose(1, 0, 2).reshape(3, device_count, own_taps).transpose(1, 0, 2)
    short_part = jnp.pad(short_part, ((0, 0), (0, 0), (0, padding))).reshape(device_count, -1)
    terms = lax.all_to_all(
        jnp.concatenate([filter_part, short_part], axis=1), ("fsdp", "ctx"), 0, 0, tiled=True
    )
    factor = 1.0 / math.sqrt(device_count * rows)
    total = jnp.sum(terms, axis=0) * factor
    filter_grad = jnp.roll(total[: own_groups * taps].reshape(own_groups, taps)[:, ::-1], 1, axis=1)
    short_grad = total[own_groups * taps :].reshape(3, own_taps + padding)[:, :own_taps]
    return (result[None], stream_grad[None], filter_grad, short_grad)


def solution(mesh):
    in_specs = (
        P("fsdp", "ctx", None),
        P("fsdp", "ctx", None),
        P(("fsdp", "ctx"), None),
        P(None, ("fsdp", "ctx")),
    )
    out_specs = (
        P("fsdp", "ctx", None),
        P("fsdp", "ctx", None),
        P(("fsdp", "ctx"), None),
        P(None, ("fsdp", "ctx")),
    )
    return jax.shard_map(
        on_device, mesh=mesh, in_specs=in_specs, out_specs=out_specs, check_vma=False
    )
```

time: 119 us -> 112 us (0.941)
  blocking collectives: 60.3 us -> 21.6 us
  waiting for transfers between devices: 0.01 us -> 17.2 us
  starting transfers between devices: 6.76 us -> 20 us
  local copies, waits for them, and re-layouts: 6.13 us -> 9.2 us
  other arithmetic: 4.29 us -> 2.42 us
    all_to_all x1 -> x0, blocking collectives: 42.1 us -> none  [on_device(): lax.all_to_all(jnp.broadcast_to(own, (device_count, own.shape[1])), ('fsd...]
    all_to_all x0 -> x1, waiting for transfers between devices: none -> 11.1 us  [on_device(): lax.all_to_all(jnp.broadcast_to(own, (device_count, own.shape[1])), ('fsd...]
    all_to_all x0 -> x1, starting transfers between devices: none -> 9.81 us  [on_device(): lax.all_to_all(jnp.broadcast_to(own, (device_count, own.shape[1])), ('fsd...]
    ppermute x2 -> x3, waiting for transfers between devices: 0.01 us -> 6.1 us  [shifted(): return lax.ppermute(value, axis, pairs)]
    ppermute x2 -> x3, starting transfers between devices: 6.76 us -> 10.2 us  [shifted(): return lax.ppermute(value, axis, pairs)]
    all_to_all x1, blocking collectives: 18.2 us -> 21.6 us  [on_device(): lax.all_to_all(jnp.concatenate([filter_part, short_part], axis=1), ('fsdp...]
    concatenate x2 -> x0, other arithmetic: 3.36 us -> none  [the longest x1 1.76 us: on_device(): jnp.concatenate([first[rows - halo:], values[rows - halo:], second[rows -...]
    slice x3 -> x1, local copies, waits for them, and re-layouts: 3.62 us -> 0.98 us  [on_device(): tails = shifted(stream[rows - 2:], 'ctx', 1)]
  transfers between devices with their start and end apart: 2 -> 4, of which waited for: 0 -> 3; matrix products, arithmetic and copies ran while one was open for 2% -> 3% of each run, Pallas kernels for 0% -> 5%
where the time goes in v2:
time: 112 us; the launch traced here: 111 us
  Pallas kernels  39.8 us (36%)
  blocking collectives  21.6 us (19%)
  starting transfers between devices  20 us (18%)
  waiting for transfers between devices  17.2 us (15%)
  local copies, waits for them, and re-layouts  9.2 us (8%)
  other arithmetic  2.42 us (2%)
    pallas_call x1, Pallas kernels, main(): pl.pallas_call(functools.partial(main_kernel, part, steps, width, rows, c...  28.7 us
    all_to_all x1, blocking collectives, on_device(): lax.all_to_all(jnp.concatenate([filter_part, short_part], axis=1), ('fsdp...  21.6 us
    all_to_all x1, waiting for transfers between devices, on_device(): lax.all_to_all(jnp.broadcast_to(own, (device_count, own.shape[1])), ('fsd...  11.1 us
    ppermute x3, starting transfers between devices, shifted(): return lax.ppermute(value, axis, pairs)  10.2 us
    all_to_all x1, starting transfers between devices, on_device(): lax.all_to_all(jnp.broadcast_to(own, (device_count, own.shape[1])), ('fsd...  9.81 us
    ppermute x3, waiting for transfers between devices, shifted(): return lax.ppermute(value, axis, pairs)  6.1 us
    pallas_call x1, Pallas kernels, edges(): pl.pallas_call(functools.partial(edge_kernel, width, taps), grid=(steps,)...  5.8 us
    pallas_call x1, Pallas kernels, toeplitz_blocks(): pl.pallas_call(functools.partial(toeplitz_kernel, taps), grid=(group_coun...  5.27 us
  transfers between devices with their start and end apart: 4, of which 3 were waited for; matrix products, arithmetic and copies ran while one was open for 3% of the time, Pallas kernels for 5%

profile of v2, /device:TPU:1, one launch (start us, length us, event | category | flops | bytes accessed | tf_op | source)
XLA Modules:
  0.0 110.9 jit_solution(4611412733610352773)
XLA Ops:
  0.6 1.0 slice_bitcast_fusion.1
  1.6 4.6 %collective-permute-start = (bf16[2,12288]{1,0:T(2,128)(2,1)S(1)}, bf16[2,12288]{1,0:T(2,128)(2,1)S(1)}, u32[]{:S(2)}, u32[]{:S(2)}) collective-permute-start(bf16[2,12288]{1,0:T(2,128)(2,1)S(1)} %slice_bitcast_fusion.1), channel_id=1, source_target_pairs={{0,1},{1,2},{2,3},{3,4},{4,5},{5,6},{6,7},{7,8},{8,9},{9,10},{10,1... | collective-permute-start | bytes 147464 | tf_op jit(solution)/shard_map/ppermute | solution.py:25
  6.2 0.7 pad_bitcast_fusion
  6.9 0.7 maximum_reduce_fusion
  7.6 0.9 broadcast_in_dim.11
  8.5 9.8 %all-to-all-start = ((f32[128,1,640]{2,1,0:T(1,128)}), f32[128,1,640]{2,1,0:T(1,128)S(1)}, u32[]{:S(2)}, u32[]{:S(2)}) async-start(f32[128,1,640]{2,1,0:T(1,128)} %broadcast_in_dim.11), calls=%async_computation | async-start | bytes 655360 | tf_op jit(solution)/shard_map/all_to_all | solution.py:362
  18.3 0.8 pad_convert_fusion.tail_a.tail_b.tail_c.refs_6_.refs_7_.refs_8_
  19.1 11.1 %all-to-all-done = f32[128,1,640]{2,1,0:T(1,128)S(1)} async-done(((f32[128,1,640]{2,1,0:T(1,128)}), f32[128,1,640]{2,1,0:T(1,128)S(1)}, u32[]{:S(2)}, u32[]{:S(2)}) %all-to-all-start) | async-done | bytes 327712 | tf_op jit(solution)/shard_map/all_to_all | solution.py:362
  30.2 0.2 copy.14
  30.4 0.1 copy.15
  30.6 0.9 reshape.52.ta_ref.tb_ref.tc_ref.refs_9_.refs_10_.refs_11_
  31.5 5.8 %edges.1 = (bf16[128,4096]{1,0:T(8,128)(2,1)}, bf16[144,4096]{1,0:T(8,128)(2,1)}) custom-call(bf16[256,12288]{1,0:T(8,128)(2,1)} %bitcast.24, bf16[256,12288]{1,0:T(8,128)(2,1)} %bitcast.25, bf16[256,12288]{1,0:T(8,128)(2,1)} %bitcast.26, bf16[256,12288]{1,0:T(8,128)(2,1)} %bitcast.27, bf16[256,12288]{1,0:T(8,128)(2,1)} %bitcast.28, ...), custom_call_target="tpu_custom_call" | custom-call | flops 10000000 | bytes 4000000 | tf_op jit(solution)/shard_map/edges/pallas_call | solution.py:129
  37.3 2.3 %collective-permute-start.2 = (bf16[144,4096]{1,0:T(8,128)(2,1)}, bf16[144,4096]{1,0:T(8,128)(2,1)S(1)}, u32[]{:S(2)}, u32[]{:S(2)}) collective-permute-start(bf16[144,4096]{1,0:T(8,128)(2,1)} %get-tuple-element.13), channel_id=1, source_target_pairs={{1,0},{2,1},{3,2},{4,3},{5,4},{6,5},{7,6},{8,7},{9,8},{10,9},{11,1... | collective-permute-start | bytes 3538952 | tf_op jit(solution)/shard_map/ppermute | solution.py:25
  39.6 3.3 %collective-permute-start.1 = (bf16[128,4096]{1,0:T(8,128)(2,1)}, bf16[128,4096]{1,0:T(8,128)(2,1)S(1)}, u32[]{:S(2)}, u32[]{:S(2)}) collective-permute-start(bf16[128,4096]{1,0:T(8,128)(2,1)} %get-tuple-element.12), channel_id=1, source_target_pairs={{0,1},{1,2},{2,3},{3,4},{4,5},{5,6},{6,7},{7,8},{8,9},{9,10},{10,1... | collective-permute-start | bytes 3145736 | tf_op jit(solution)/shard_map/ppermute | solution.py:25
  42.9 0.1 copy.16
  43.0 0.7 reshape.53.filters_ref
  43.6 5.3 %toeplitz_blocks.1 = (bf16[8192,256]{1,0:T(8,128)(2,1)}, bf16[8192,256]{1,0:T(8,128)(2,1)}) custom-call(f32[256,128]{1,0:T(8,128)} %reshape.53.filters_ref, bf16[128,128]{1,0:T(8,128)(2,1)} %constant.10.clone.turn_ref), custom_call_target="tpu_custom_call" | custom-call | flops 1000000000 | bytes 10000000 | tf_op jit(solution)/shard_map/toeplitz_blocks/pallas_call | solution.py:72
  48.9 6.0 %collective-permute-done.1.refs_4_ = bf16[128,4096]{1,0:T(8,128)(2,1)S(1)} collective-permute-done((bf16[128,4096]{1,0:T(8,128)(2,1)}, bf16[128,4096]{1,0:T(8,128)(2,1)S(1)}, u32[]{:S(2)}, u32[]{:S(2)}) %collective-permute-start.1) | collective-permute-done | bytes 1048608 | tf_op jit(solution)/shard_map/ppermute | solution.py:25
  54.9 0.1 collective-permute-done.2.refs_5_
  55.0 0.8 copy-done.1
  55.9 0.5 copy-done
  56.3 28.7 %hyena_main.1 = (bf16[256,4096]{1,0:T(8,128)(2,1)}, bf16[256,12288]{1,0:T(8,128)(2,1)}, f32[256,128]{1,0:T(8,128)}, f32[3,3,4096]{2,1,0:T(4,128)}) custom-call(bf16[256,12288]{1,0:T(8,128)(2,1)} %bitcast.32, bf16[256,12288]{1,0:T(8,128)(2,1)} %bitcast.33, bf16[256,12288]{1,0:T(8,128)(2,1)} %bitcast.34, bf16[256,4096]{1,0:T(8,128)(2,1)} %bitcast.37, ...), custom_call_target="tpu_custom_call" | custom-call | flops 10000000000 | bytes 20000000 | tf_op jit(solution)/shard_map/hyena_main/pallas_call | solution.py:308
  85.0 0.9 reshape.54
  86.0 1.0 copy.17
  87.1 0.2 reshape.55
  87.3 0.1 copy.21
  87.4 0.2 copy.20
  87.6 21.6 %all_to_all.18 = f32[128,1,640]{2,1,0:T(1,128)S(1)} all-to-all(f32[128,1,640]{2,1,0:T(1,128)S(1)} %copy.20), channel_id=1, replica_groups=mesh['fsdp'=8,'ctx'=16] {'fsdp','ctx'}, dimensions={0} | all-to-all | bytes 655360 | tf_op jit(solution)/shard_map/all_to_all | solution.py:387
  109.3 0.2 reduce_sum.9
  109.6 0.6 slice.45
  110.2 0.1 slice.44
  110.3 0.6 pad_maximum_fusion
  (13 shorter events, 0.3 us)
Async XLA Ops:
  1.6 16.7 %collective-permute-start = (bf16[2,12288]{1,0:T(2,128)(2,1)S(1)}, bf16[2,12288]{1,0:T(2,128)(2,1)S(1)}, u32[]{:S(2)}, u32[]{:S(2)}) collective-permute-start(bf16[2,12288]{1,0:T(2,128)(2,1)S(1)} %slice_bitcast_fusion.1), channel_id=1, source_target_pairs={{0,1},{1,2},{2,3},{3,4},{4,5},{5,6},{6,7},{7,8},{8,9},{9,10},{10,1... | collective-permute-start | bytes 147464 | tf_op jit(solution)/shard_map/ppermute | solution.py:25
  8.5 21.7 %all-to-all-start = ((f32[128,1,640]{2,1,0:T(1,128)}), f32[128,1,640]{2,1,0:T(1,128)S(1)}, u32[]{:S(2)}, u32[]{:S(2)}) async-start(f32[128,1,640]{2,1,0:T(1,128)} %broadcast_in_dim.11), calls=%async_computation | async-start | bytes 655360 | tf_op jit(solution)/shard_map/all_to_all | solution.py:362
  37.3 17.7 %collective-permute-start.2 = (bf16[144,4096]{1,0:T(8,128)(2,1)}, bf16[144,4096]{1,0:T(8,128)(2,1)S(1)}, u32[]{:S(2)}, u32[]{:S(2)}) collective-permute-start(bf16[144,4096]{1,0:T(8,128)(2,1)} %get-tuple-element.13), channel_id=1, source_target_pairs={{1,0},{2,1},{3,2},{4,3},{5,4},{6,5},{7,6},{8,7},{9,8},{10,9},{11,1... | collective-permute-start | bytes 3538952 | tf_op jit(solution)/shard_map/ppermute | solution.py:25
  39.6 15.3 %collective-permute-start.1 = (bf16[128,4096]{1,0:T(8,128)(2,1)}, bf16[128,4096]{1,0:T(8,128)(2,1)S(1)}, u32[]{:S(2)}, u32[]{:S(2)}) collective-permute-start(bf16[128,4096]{1,0:T(8,128)(2,1)} %get-tuple-element.12), channel_id=1, source_target_pairs={{0,1},{1,2},{2,3},{3,4},{4,5},{5,6},{6,7},{7,8},{8,9},{9,10},{10,1... | collective-permute-start | bytes 3145736 | tf_op jit(solution)/shard_map/ppermute | solution.py:25
  54.9 1.0 copy-start.1
  55.0 1.3 %copy-start = (bf16[144,4096]{1,0:T(8,128)(2,1)}, bf16[144,4096]{1,0:T(8,128)(2,1)S(1)}, u32[]{:S(2)}) copy-start(bf16[144,4096]{1,0:T(8,128)(2,1)S(1)} %collective-permute-done.2.refs_5_) | copy-start | bytes 3538948

commit v3 on v2

--- a/solution.py
+++ b/solution.py
@@ -16,7 +16,8 @@
 PITCH = BLOCK + 8
 LEAD = 8
 PARTS = 1
-VMEM = 56 * 1024 * 1024
+VMEM = 24 * 1024 * 1024
+MAIN_VMEM = 24 * 1024 * 1024
 
 
 def shifted(value, axis, by):
@@ -153,13 +154,47 @@
     )(*[stream] * 8, cot, cot, *[tails] * 3, *[tap_rows] * 3)
 
 
+def gates_kernel(width, rows, second_ref, tail_b, cot_ref, tb_ref, fb_ref, gated_ref, xb):
+    for part in range(width // LANES):
+        lanes = slice(part * LANES, (part + 1) * LANES)
+        x = xb.at[part]
+        (tap_b,) = taps_of((tb_ref,), lanes)
+        x[:LEAD] = tail_b[:, lanes]
+        x[LEAD:] = second_ref[:, lanes].astype(F32)
+        for r in range(0, rows, PACK):
+            b = featurized(x, LEAD + r, PACK, tap_b)
+            fb_ref[r : r + PACK, lanes] = b
+            gated_ref[r : r + PACK, lanes] = (b.astype(F32) * cot_ref[r : r + PACK, lanes].astype(F32)).astype(BF16)
+
+
+def gates(stream, cot, tails, tap_rows, width=8 * LANES):
+    rows, channels = cot.shape
+    steps = channels // width
+
+    def column(which, height):
+        return pl.BlockSpec((height, width), lambda j: (0, which * steps + j))
+
+    shape = jax.ShapeDtypeStruct((rows, channels), BF16)
+    return pl.pallas_call(
+        functools.partial(gates_kernel, width, rows),
+        grid=(steps,),
+        in_specs=[column(1, rows), column(1, LEAD), column(0, rows), column(1, 3)],
+        out_specs=[column(0, rows)] * 2,
+        out_shape=[shape, shape],
+        scratch_shapes=[pltpu.VMEM((width // LANES, LEAD + rows, LANES), F32)],
+        compiler_params=pltpu.CompilerParams(vmem_limit_bytes=VMEM),
+        cost_estimate=pl.CostEstimate(flops=10**7, bytes_accessed=8 * 10**6, transcendentals=0),
+        name="gates",
+    )(stream, tails, cot, tap_rows)
+
+
 def main_kernel(
     part, steps, width, rows, channels, taps, per_group, aliased, *refs
 ):
-    (first_ref, second_ref, values_ref, cot_ref, before_ref, after_ref, tail_a, tail_b, tail_c,
-     ta_ref, tb_ref, tc_ref, ahead, behind) = refs[:14]
-    result_ref, grad_ref, fgrad_ref, sgrad_ref = refs[14 + aliased : 18 + aliased]
-    *buffers, wheels, held, sems = refs[18 + aliased :]
+    (first_ref, second_ref, values_ref, cot_ref, before_ref, after_ref, fb_ref, gated_ref, tail_a, tail_c,
+     ta_ref, tb_ref, tc_ref, ahead, behind) = refs[:15]
+    result_ref, grad_ref, fgrad_ref, sgrad_ref = refs[15 + aliased : 19 + aliased]
+    *buffers, wheels, held, sems = refs[19 + aliased :]
     step = pl.program_id(0)
     groups = LANES // per_group
     blocks = rows // BLOCK
@@ -182,9 +217,9 @@
 
     def inner(p):
         lanes = slice(p * LANES, (p + 1) * LANES)
-        xa, xb, xc, fa, fb, fc, mixed, gated, fga, fgb, fgc, masked, tile = (ref.at[p] for ref in buffers)
+        xa, xc, fa, fc, mixed, gated, fga, fgb, fgc, masked, tile = (ref.at[p] for ref in buffers)
         tap_a, tap_b, tap_c = taps_of((ta_ref, tb_ref, tc_ref), lanes)
-        for x, lead, own in ((xa, tail_a, first_ref), (xb, tail_b, second_ref), (xc, tail_c, values_ref)):
+        for x, lead, own in ((xa, tail_a, first_ref), (xc, tail_c, values_ref)):
             x[:LEAD] = lead[:, lanes]
             x[LEAD:] = own[:, lanes].astype(F32)
         tile[:PACK] = after_ref[taps:, lanes].astype(F32)
@@ -198,10 +233,7 @@
             fa[r : r + PACK] = a
             fc[r : r + PACK] = c
         mixed[taps + rows :] = (tile[1 : 1 + PACK] * tile[3 : 3 + PACK]).astype(BF16)
-        for r in range(0, rows, PACK):
-            b = featurized(xb, LEAD + r, PACK, tap_b)
-            fb[r : r + PACK] = b
-            gated[r : r + PACK] = (b.astype(F32) * cot_ref[r : r + PACK, lanes].astype(F32)).astype(BF16)
+        gated[:rows] = gated_ref[:, lanes]
         gated[rows : rows + taps] = after_ref[:taps, lanes]
         gated[rows + taps :] = jnp.where(row[:PACK] == 0, tile[:PACK], 0.0).astype(BF16)
 
@@ -213,7 +245,7 @@
             for i in range(2):
                 at = slice((b + i) * BLOCK, (b + i + 1) * BLOCK)
                 hidden = pick_groups(product[:, i * LANES : (i + 1) * LANES], BLOCK, per_group)
-                result_ref[at, lanes] = (fb[at].astype(F32) * hidden).astype(BF16)
+                result_ref[at, lanes] = (fb_ref[at, lanes].astype(F32) * hidden).astype(BF16)
                 fgb[at] = cot_ref[at, lanes].astype(F32) * hidden
         heads = [slice(top + g * BLOCK, top + g * BLOCK + PACK) for g in range(groups)]
         product = jnp.dot(
@@ -257,13 +289,13 @@
             wheels[start : start + BLOCK] = jnp.where(col > row, moment[at, :taps], later)
 
         column = pl.multiple_of(step * width + p * LANES, LANES)
-        for which, (fg, x, tap) in enumerate(((fga, xa, tap_a), (fgb, xb, tap_b), (fgc, xc, tap_c))):
+        for which, (fg, x, tap) in enumerate(((fga, xa, tap_a), (fgb, None, tap_b), (fgc, xc, tap_c))):
             sums = [jnp.zeros((8, LANES), F32) for _ in range(3)]
             for r in range(0, rows, PACK):
                 near = [fg[pl.ds(r + s, PACK)] for s in range(3)]
                 grad = tap[0] * near[0] + tap[1] * near[1] + tap[2] * near[2]
                 held[r : r + PACK, pl.ds(which * steps * width + column, LANES)] = grad.astype(BF16)
-                own = x[LEAD + r : LEAD + r + PACK]
+                own = second_ref[r : r + PACK, lanes].astype(F32) if x is None else x[LEAD + r : LEAD + r + PACK]
                 for s in range(3):
                     term = near[s] * own
                     sums[s] = sums[s] + (term[:8] + term[8:])
@@ -288,7 +320,7 @@
             copy(which, 0, steps * width).wait()
 
 
-def main(part, stream, cot, before, after, tails, tap_rows, ahead, behind, earlier, taps, per_group, width=2 * LANES):
+def main(part, stream, cot, before, after, fb, gated, tails, tap_rows, ahead, behind, earlier, taps, per_group, width=2 * LANES):
     rows, channels = cot.shape
     all_steps = channels // width
     steps = all_steps // PARTS
@@ -309,8 +341,8 @@
         functools.partial(main_kernel, part, steps, width, rows, channels, taps, per_group, len(earlier)),
         grid=(steps,),
         in_specs=[column(w, rows) for w in range(3)]
-        + [column(0, rows), own(taps), own(taps + PACK)]
-        + [column(w, LEAD) for w in range(3)]
+        + [column(0, rows), own(taps), own(taps + PACK), column(0, rows), column(0, rows)]
+        + [column(w, LEAD) for w in (0, 2)]
         + [column(w, 3) for w in range(3)]
         + [table, table]
         + [pl.BlockSpec(memory_space=pl.ANY)] * len(earlier),
@@ -325,8 +357,8 @@
             jax.ShapeDtypeStruct((steps * groups, taps), F32),
             jax.ShapeDtypeStruct((3, 3, steps * width), F32),
         ],
-        scratch_shapes=[pltpu.VMEM((inner, LEAD + rows, LANES), F32)] * 3
-        + [pltpu.VMEM((inner, rows, LANES), BF16)] * 3
+        scratch_shapes=[pltpu.VMEM((inner, LEAD + rows, LANES), F32)] * 2
+        + [pltpu.VMEM((inner, rows, LANES), BF16)] * 2
         + [pltpu.VMEM((inner, taps + rows + PACK, LANES), BF16)] * 2
         + [pltpu.VMEM((inner, rows + PACK, LANES), F32)] * 3
         + [
@@ -336,11 +368,11 @@
             pltpu.VMEM((rows, 3 * steps * width), BF16),
             pltpu.SemaphoreType.DMA((3,)),
         ],
-        input_output_aliases={14 + i: i for i in range(len(earlier))},
-        compiler_params=pltpu.CompilerParams(vmem_limit_bytes=VMEM),
+        input_output_aliases={15 + i: i for i in range(len(earlier))},
+        compiler_params=pltpu.CompilerParams(vmem_limit_bytes=MAIN_VMEM),
         cost_estimate=pl.CostEstimate(flops=10**10, bytes_accessed=2 * 10**7, transcendentals=0),
         name="hyena_main",
-    )(*[stream] * 3, cot, before, after, *[tails] * 3, *[tap_rows] * 3, ahead, behind, *earlier)
+    )(*[stream] * 3, cot, before, after, fb, gated, *[tails] * 2, *[tap_rows] * 3, ahead, behind, *earlier)
 
 
 def on_device(streams, cotangent, filters, short_taps):
@@ -371,10 +403,11 @@
         mixed_tail, gated_head = edges(part, stream, cot, tails, whole_taps, taps)
         halos.append((shifted(mixed_tail, "ctx", 1), shifted(gated_head, "ctx", -1)))
     ahead, behind = toeplitz_blocks(whole_filters)
+    fb, gated = gates(stream, cot, tails, whole_taps)
     earlier, filter_parts, short_parts = (), [], []
     for part in range(PARTS):
         result, stream_grad, filter_part, short_part = main(
-            part, stream, cot, *halos[part], tails, whole_taps, ahead, behind, earlier, taps, per_group
+            part, stream, cot, *halos[part], fb, gated, tails, whole_taps, ahead, behind, earlier, taps, per_group
         )
         earlier = (result, stream_grad)
         filter_parts.append(filter_part)

time: 112 us -> 109 us (0.973)
  Pallas kernels: 39.8 us -> 37.5 us
  local copies, waits for them, and re-layouts: 9.2 us -> 10.4 us
    unnamed x7 -> x13, local copies, waits for them, and re-layouts: 2.12 us -> 6.38 us
    pallas_call x1, Pallas kernels: 5.27 us -> 2.24 us  [toeplitz_blocks(): pl.pallas_call(functools.partial(toeplitz_kernel, taps), grid=(group_coun...]
    pallas_call x0 -> x1, Pallas kernels: none -> 2.65 us  [gates(): pl.pallas_call(functools.partial(gates_kernel, width, rows), grid=(steps,...]
    pallas_call x1, Pallas kernels: 5.8 us -> 3.99 us  [edges(): pl.pallas_call(functools.partial(edge_kernel, width, taps), grid=(steps,)...]
    ppermute x3, waiting for transfers between devices: 6.1 us -> 4.41 us  [shifted(): return lax.ppermute(value, axis, pairs)]
  transfers between devices with their start and end apart: 4 -> 4, of which waited for: 3 -> 3; matrix products, arithmetic and copies ran while one was open for 3% -> 2% of each run, Pallas kernels for 5% -> 5%
where the time goes in v3:
time: 109 us; the launch traced here: 108 us
  Pallas kernels  37.5 us (34%)
  blocking collectives  21.5 us (20%)
  starting transfers between devices  20 us (18%)
  waiting for transfers between devices  16.2 us (15%)
  local copies, waits for them, and re-layouts  10.4 us (10%)
  other arithmetic  1.66 us (2%)
    pallas_call x1, Pallas kernels, main(): pl.pallas_call(functools.partial(main_kernel, part, steps, width, rows, c...  28.6 us
    all_to_all x1, blocking collectives, on_device(): lax.all_to_all(jnp.concatenate([filter_part, short_part], axis=1), ('fsdp...  21.5 us
    all_to_all x1, waiting for transfers between devices, on_device(): lax.all_to_all(jnp.broadcast_to(own, (device_count, own.shape[1])), ('fsd...  11.8 us
    ppermute x3, starting transfers between devices, shifted(): return lax.ppermute(value, axis, pairs)  10.1 us
    all_to_all x1, starting transfers between devices, on_device(): lax.all_to_all(jnp.broadcast_to(own, (device_count, own.shape[1])), ('fsd...  9.81 us
    unnamed x13, local copies, waits for them, and re-layouts  6.38 us
    ppermute x3, waiting for transfers between devices, shifted(): return lax.ppermute(value, axis, pairs)  4.41 us
    pallas_call x1, Pallas kernels, edges(): pl.pallas_call(functools.partial(edge_kernel, width, taps), grid=(steps,)...  3.99 us
  transfers between devices with their start and end apart: 4, of which 3 were waited for; matrix products, arithmetic and copies ran while one was open for 2% of the time, Pallas kernels for 5%

profile of v3, /device:TPU:1, one launch (start us, length us, event | category | flops | bytes accessed | tf_op | source)
XLA Modules:
  0.0 108.1 jit_solution(4237888845306281578)
XLA Ops:
  0.6 1.1 %slice_bitcast_fusion.1 = bf16[2,12288]{1,0:T(2,128)(2,1)S(1)} fusion(bf16[1,256,12288]{2,1,0:T(8,128)(2,1)} %param.5), kind=kLoop, calls=%fused_computation.3 | loop fusion | bytes 98304 | tf_op jit(solution)/shard_map/slice | solution.py:387
  1.8 4.6 %collective-permute-start = (bf16[2,12288]{1,0:T(2,128)(2,1)S(1)}, bf16[2,12288]{1,0:T(2,128)(2,1)S(1)}, u32[]{:S(2)}, u32[]{:S(2)}) collective-permute-start(bf16[2,12288]{1,0:T(2,128)(2,1)S(1)} %slice_bitcast_fusion.1), channel_id=1, source_target_pairs={{0,1},{1,2},{2,3},{3,4},{4,5},{5,6},{6,7},{7,8},{8,9},{9,10},{10,1... | collective-permute-start | bytes 147464 | tf_op jit(solution)/shard_map/ppermute | solution.py:26
  6.4 0.7 pad_bitcast_fusion
  7.1 0.7 maximum_reduce_fusion
  7.8 0.9 broadcast_in_dim.11
  8.7 9.8 %all-to-all-start = ((f32[128,1,640]{2,1,0:T(1,128)}), f32[128,1,640]{2,1,0:T(1,128)S(1)}, u32[]{:S(2)}, u32[]{:S(2)}) async-start(f32[128,1,640]{2,1,0:T(1,128)} %broadcast_in_dim.11), calls=%async_computation | async-start | bytes 655360 | tf_op jit(solution)/shard_map/all_to_all | solution.py:394
  18.6 11.8 %all-to-all-done = f32[128,1,640]{2,1,0:T(1,128)S(1)} async-done(((f32[128,1,640]{2,1,0:T(1,128)}), f32[128,1,640]{2,1,0:T(1,128)S(1)}, u32[]{:S(2)}, u32[]{:S(2)}) %all-to-all-start) | async-done | bytes 327712 | tf_op jit(solution)/shard_map/all_to_all | solution.py:394
  30.4 0.2 copy.14
  30.6 0.1 copy.15
  30.7 0.2 reshape.52.ta_ref.tb_ref.tc_ref.refs_10_.refs_11_.refs_12_
  31.0 2.8 %copy-done = bf16[1,256,12288]{2,1,0:T(8,128)(2,1)S(1)} copy-done((bf16[1,256,12288]{2,1,0:T(8,128)(2,1)S(1)}, bf16[1,256,12288]{2,1,0:T(8,128)(2,1)}, u32[]{:S(2)}) %copy-start) | copy-done | bytes 6291480
  33.7 4.0 %edges.1 = (bf16[128,4096]{1,0:T(8,128)(2,1)}, bf16[144,4096]{1,0:T(8,128)(2,1)}) custom-call(bf16[256,12288]{1,0:T(8,128)(2,1)S(1)} %bitcast.24, bf16[256,12288]{1,0:T(8,128)(2,1)S(1)} %bitcast.25, bf16[256,12288]{1,0:T(8,128)(2,1)S(1)} %bitcast.26, bf16[256,12288]{1,0:T(8,128)(2,1)S(1)} %bitcast.27, bf16[256,12288]{1,0:T(8,128)(2,1)S(1)} %bitcast.28, ...), custom_call_target="tpu_custom_call" | custom-call | flops 10000000 | bytes 4000000 | tf_op jit(solution)/shard_map/edges/pallas_call | solution.py:130
  37.7 2.3 %collective-permute-start.2 = (bf16[144,4096]{1,0:T(8,128)(2,1)}, bf16[144,4096]{1,0:T(8,128)(2,1)}, u32[]{:S(2)}, u32[]{:S(2)}) collective-permute-start(bf16[144,4096]{1,0:T(8,128)(2,1)} %get-tuple-element.15), channel_id=1, source_target_pairs={{1,0},{2,1},{3,2},{4,3},{5,4},{6,5},{7,6},{8,7},{9,8},{10,9},{11,1... | collective-permute-start | bytes 3538952 | tf_op jit(solution)/shard_map/ppermute | solution.py:26
  40.0 3.3 %collective-permute-start.1 = (bf16[128,4096]{1,0:T(8,128)(2,1)}, bf16[128,4096]{1,0:T(8,128)(2,1)}, u32[]{:S(2)}, u32[]{:S(2)}) collective-permute-start(bf16[128,4096]{1,0:T(8,128)(2,1)} %get-tuple-element.14), channel_id=1, source_target_pairs={{0,1},{1,2},{2,3},{3,4},{4,5},{5,6},{6,7},{7,8},{8,9},{9,10},{10,1... | collective-permute-start | bytes 3145736 | tf_op jit(solution)/shard_map/ppermute | solution.py:26
  43.3 0.1 copy.16
  43.4 2.8 %copy-done.1 = bf16[1,256,12288]{2,1,0:T(8,128)(2,1)S(1)} copy-done((bf16[1,256,12288]{2,1,0:T(8,128)(2,1)S(1)}, bf16[1,256,12288]{2,1,0:T(8,128)(2,1)}, u32[]{:S(2)}) %copy-start.1) | copy-done | bytes 6291480
  46.2 2.7 %gates.1 = (bf16[256,4096]{1,0:T(8,128)(2,1)S(1)}, bf16[256,4096]{1,0:T(8,128)(2,1)S(1)}) custom-call(bf16[256,12288]{1,0:T(8,128)(2,1)S(1)} %bitcast.32, f32[8,12288]{1,0:T(8,128)S(1)} %pad_convert_fusion.tail_a.tail_b.tail_c.refs_8_.refs_9_, bf16[256,4096]{1,0:T(8,128)(2,1)S(1)} %bitcast.38, ...), custom_call_target="tpu_custom_call" | custom-call | flops 10000000 | bytes 8000000 | tf_op jit(solution)/shard_map/gates/pallas_call | solution.py:178
  48.9 2.2 %toeplitz_blocks.1 = (bf16[8192,256]{1,0:T(8,128)(2,1)S(1)}, bf16[8192,256]{1,0:T(8,128)(2,1)S(1)}) custom-call(f32[256,128]{1,0:T(8,128)S(1)} %reshape.53.filters_ref, bf16[128,128]{1,0:T(8,128)(2,1)S(1)} %copy-done.4), custom_call_target="tpu_custom_call" | custom-call | flops 1000000000 | bytes 10000000 | tf_op jit(solution)/shard_map/toeplitz_blocks/pallas_call | solution.py:73
  51.1 4.2 %collective-permute-done.1.refs_4_ = bf16[128,4096]{1,0:T(8,128)(2,1)} collective-permute-done((bf16[128,4096]{1,0:T(8,128)(2,1)}, bf16[128,4096]{1,0:T(8,128)(2,1)}, u32[]{:S(2)}, u32[]{:S(2)}) %collective-permute-start.1) | collective-permute-done | bytes 1048608 | tf_op jit(solution)/shard_map/ppermute | solution.py:26
  55.3 0.2 collective-permute-done.2.refs_5_
  55.6 28.6 %hyena_main.1 = (bf16[256,4096]{1,0:T(8,128)(2,1)}, bf16[256,12288]{1,0:T(8,128)(2,1)}, f32[256,128]{1,0:T(8,128)S(1)}, f32[3,3,4096]{2,1,0:T(4,128)S(1)}) custom-call(bf16[256,12288]{1,0:T(8,128)(2,1)S(1)} %bitcast.33, bf16[256,12288]{1,0:T(8,128)(2,1)S(1)} %bitcast.34, bf16[256,12288]{1,0:T(8,128)(2,1)S(1)} %bitcast.35, bf16[256,4096]{1,0:T(8,128)(2,1)S(1)} %bitcast.39, ...), custom_call_target="tpu_custom_call" | custom-call | flops 10000000000 | bytes 20000000 | tf_op jit(solution)/shard_map/hyena_main/pallas_call | solution.py:340
  84.2 0.1 copy.19
  84.3 0.1 copy.17
  84.4 0.2 reshape.55
  84.6 0.1 copy.21
  84.8 0.2 copy.20
  85.0 21.5 %all_to_all.18 = f32[128,1,640]{2,1,0:T(1,128)S(1)} all-to-all(f32[128,1,640]{2,1,0:T(1,128)S(1)} %copy.20), channel_id=1, replica_groups=mesh['fsdp'=8,'ctx'=16] {'fsdp','ctx'}, dimensions={0} | all-to-all | bytes 655360 | tf_op jit(solution)/shard_map/all_to_all | solution.py:420
  106.5 0.2 reduce_sum.9
  106.8 0.1 slice.43
  106.8 0.6 slice.45
  107.4 0.1 slice.44
  107.5 0.6 pad_maximum_fusion
  (20 shorter events, 0.2 us)
Async XLA Ops:
  0.6 30.3 %copy-start.3 = (bf16[1,256,4096]{2,1,0:T(8,128)(2,1)S(1)}, bf16[1,256,4096]{2,1,0:T(8,128)(2,1)}, u32[]{:S(2)}) copy-start(bf16[1,256,4096]{2,1,0:T(8,128)(2,1)} %param.6) | copy-start | bytes 6291460
  1.8 16.7 %collective-permute-start = (bf16[2,12288]{1,0:T(2,128)(2,1)S(1)}, bf16[2,12288]{1,0:T(2,128)(2,1)S(1)}, u32[]{:S(2)}, u32[]{:S(2)}) collective-permute-start(bf16[2,12288]{1,0:T(2,128)(2,1)S(1)} %slice_bitcast_fusion.1), channel_id=1, source_target_pairs={{0,1},{1,2},{2,3},{3,4},{4,5},{5,6},{6,7},{7,8},{8,9},{9,10},{10,1... | collective-permute-start | bytes 147464 | tf_op jit(solution)/shard_map/ppermute | solution.py:26
  8.7 21.7 %all-to-all-start = ((f32[128,1,640]{2,1,0:T(1,128)}), f32[128,1,640]{2,1,0:T(1,128)S(1)}, u32[]{:S(2)}, u32[]{:S(2)}) async-start(f32[128,1,640]{2,1,0:T(1,128)} %broadcast_in_dim.11), calls=%async_computation | async-start | bytes 655360 | tf_op jit(solution)/shard_map/all_to_all | solution.py:394
  30.9 2.8 %copy-start = (bf16[1,256,12288]{2,1,0:T(8,128)(2,1)S(1)}, bf16[1,256,12288]{2,1,0:T(8,128)(2,1)}, u32[]{:S(2)}) copy-start(bf16[1,256,12288]{2,1,0:T(8,128)(2,1)} %param.5) | copy-start | bytes 18874372
  37.7 17.8 %collective-permute-start.2 = (bf16[144,4096]{1,0:T(8,128)(2,1)}, bf16[144,4096]{1,0:T(8,128)(2,1)}, u32[]{:S(2)}, u32[]{:S(2)}) collective-permute-start(bf16[144,4096]{1,0:T(8,128)(2,1)} %get-tuple-element.15), channel_id=1, source_target_pairs={{1,0},{2,1},{3,2},{4,3},{5,4},{6,5},{7,6},{8,7},{9,8},{10,9},{11,1... | collective-permute-start | bytes 3538952 | tf_op jit(solution)/shard_map/ppermute | solution.py:26
  40.0 15.3 %collective-permute-start.1 = (bf16[128,4096]{1,0:T(8,128)(2,1)}, bf16[128,4096]{1,0:T(8,128)(2,1)}, u32[]{:S(2)}, u32[]{:S(2)}) collective-permute-start(bf16[128,4096]{1,0:T(8,128)(2,1)} %get-tuple-element.14), channel_id=1, source_target_pairs={{0,1},{1,2},{2,3},{3,4},{4,5},{5,6},{6,7},{7,8},{8,9},{9,10},{10,1... | collective-permute-start | bytes 3145736 | tf_op jit(solution)/shard_map/ppermute | solution.py:26
  43.4 2.8 %copy-start.1 = (bf16[1,256,12288]{2,1,0:T(8,128)(2,1)S(1)}, bf16[1,256,12288]{2,1,0:T(8,128)(2,1)}, u32[]{:S(2)}) copy-start(bf16[1,256,12288]{2,1,0:T(8,128)(2,1)} %param.5) | copy-start | bytes 18874372
  46.2 2.7 %copy-start.4 = (bf16[128,128]{1,0:T(8,128)(2,1)S(1)}, bf16[128,128]{1,0:T(8,128)(2,1)}, u32[]{:S(2)}) copy-start(bf16[128,128]{1,0:T(8,128)(2,1)} %constant.10.clone.turn_ref) | copy-start | bytes 98308
  46.2 9.3 %copy-start.2 = (bf16[1,256,12288]{2,1,0:T(8,128)(2,1)S(1)}, bf16[1,256,12288]{2,1,0:T(8,128)(2,1)}, u32[]{:S(2)}) copy-start(bf16[1,256,12288]{2,1,0:T(8,128)(2,1)} %param.5) | copy-start | bytes 18874372

commit v4 on v3

--- a/solution.py
+++ b/solution.py
@@ -17,7 +17,8 @@
 LEAD = 8
 PARTS = 1
 VMEM = 24 * 1024 * 1024
-MAIN_VMEM = 24 * 1024 * 1024
+EDGE_VMEM = 61 * 1024 * 1024
+MAIN_VMEM = 46 * 1024 * 1024
 
 
 def shifted(value, axis, by):
@@ -148,7 +149,7 @@
             pltpu.VMEM((LEAD + PACK, LANES), F32),
             pltpu.VMEM((PACK, LANES), F32),
         ],
-        compiler_params=pltpu.CompilerParams(vmem_limit_bytes=VMEM),
+        compiler_params=pltpu.CompilerParams(vmem_limit_bytes=EDGE_VMEM),
         cost_estimate=pl.CostEstimate(flops=10**7, bytes_accessed=4 * 10**6, transcendentals=0),
         name="edges",
     )(*[stream] * 8, cot, cot, *[tails] * 3, *[tap_rows] * 3)

time: 109 us -> 108 us (level)
  waiting for transfers between devices: 16.2 us -> 11.5 us
  local copies, waits for them, and re-layouts: 10.4 us -> 12.1 us
  Pallas kernels: 37.5 us -> 39.1 us
    ppermute x3, waiting for transfers between devices: 4.41 us -> 0.45 us  [shifted(): return lax.ppermute(value, axis, pairs)]
    pallas_call x1, Pallas kernels: 3.99 us -> 5.92 us  [edges(): pl.pallas_call(functools.partial(edge_kernel, width, taps), grid=(steps,)...]
    unnamed x13 -> x19, local copies, waits for them, and re-layouts: 6.38 us -> 7.53 us
  transfers between devices with their start and end apart: 4 -> 4, of which waited for: 3 -> 3; matrix products, arithmetic and copies ran while one was open for 2% -> 3% of each run, Pallas kernels for 5% -> 5%
where the time goes in v4:
time: 108 us; the launch traced here: 107 us
  Pallas kernels  39.1 us (36%)
  blocking collectives  21.5 us (20%)
  starting transfers between devices  20 us (19%)
  local copies, waits for them, and re-layouts  12.1 us (11%)
  waiting for transfers between devices  11.5 us (11%)
  other arithmetic  2.4 us (2%)
    pallas_call x1, Pallas kernels, main(): pl.pallas_call(functools.partial(main_kernel, part, steps, width, rows, c...  28.3 us
    all_to_all x1, blocking collectives, on_device(): lax.all_to_all(jnp.concatenate([filter_part, short_part], axis=1), ('fsdp...  21.5 us
    all_to_all x1, waiting for transfers between devices, on_device(): lax.all_to_all(jnp.broadcast_to(own, (device_count, own.shape[1])), ('fsd...  11.1 us
    ppermute x3, starting transfers between devices, shifted(): return lax.ppermute(value, axis, pairs)  10.2 us
    all_to_all x1, starting transfers between devices, on_device(): lax.all_to_all(jnp.broadcast_to(own, (device_count, own.shape[1])), ('fsd...  9.81 us
    unnamed x19, local copies, waits for them, and re-layouts  7.53 us
    pallas_call x1, Pallas kernels, edges(): pl.pallas_call(functools.partial(edge_kernel, width, taps), grid=(steps,)...  5.92 us
    pallas_call x1, Pallas kernels, gates(): pl.pallas_call(functools.partial(gates_kernel, width, rows), grid=(steps,...  2.65 us
  transfers between devices with their start and end apart: 4, of which 3 were waited for; matrix products, arithmetic and copies ran while one was open for 3% of the time, Pallas kernels for 5%

profile of v4, /device:TPU:1, one launch (start us, length us, event | category | flops | bytes accessed | tf_op | source)
XLA Modules:
  0.0 107.4 jit_solution(14477764793628834492)
XLA Ops:
  0.6 1.0 slice_bitcast_fusion.1
  1.6 4.6 %collective-permute-start = (bf16[2,12288]{1,0:T(2,128)(2,1)S(1)}, bf16[2,12288]{1,0:T(2,128)(2,1)S(1)}, u32[]{:S(2)}, u32[]{:S(2)}) collective-permute-start(bf16[2,12288]{1,0:T(2,128)(2,1)S(1)} %slice_bitcast_fusion.1), channel_id=1, source_target_pairs={{0,1},{1,2},{2,3},{3,4},{4,5},{5,6},{6,7},{7,8},{8,9},{9,10},{10,1... | collective-permute-start | bytes 147464 | tf_op jit(solution)/shard_map/ppermute | solution.py:27
  6.2 0.7 pad_bitcast_fusion
  6.9 0.7 maximum_reduce_fusion
  7.6 0.9 broadcast_in_dim.11
  8.5 9.8 %all-to-all-start = ((f32[128,1,640]{2,1,0:T(1,128)}), f32[128,1,640]{2,1,0:T(1,128)S(1)}, u32[]{:S(2)}, u32[]{:S(2)}) async-start(f32[128,1,640]{2,1,0:T(1,128)} %broadcast_in_dim.11), calls=%async_computation | async-start | bytes 655360 | tf_op jit(solution)/shard_map/all_to_all | solution.py:395
  18.3 0.8 pad_convert_fusion.tail_a.tail_b.tail_c.refs_8_.refs_9_
  19.1 11.1 %all-to-all-done = f32[128,1,640]{2,1,0:T(1,128)S(1)} async-done(((f32[128,1,640]{2,1,0:T(1,128)}), f32[128,1,640]{2,1,0:T(1,128)S(1)}, u32[]{:S(2)}, u32[]{:S(2)}) %all-to-all-start) | async-done | bytes 327712 | tf_op jit(solution)/shard_map/all_to_all | solution.py:395
  30.2 0.2 copy.14
  30.4 0.1 copy.15
  30.6 0.9 reshape.52.ta_ref.tb_ref.tc_ref.refs_10_.refs_11_.refs_12_
  31.5 5.9 %edges.1 = (bf16[128,4096]{1,0:T(8,128)(2,1)}, bf16[144,4096]{1,0:T(8,128)(2,1)}) custom-call(bf16[256,12288]{1,0:T(8,128)(2,1)} %bitcast.24, bf16[256,12288]{1,0:T(8,128)(2,1)} %bitcast.25, bf16[256,12288]{1,0:T(8,128)(2,1)} %bitcast.26, bf16[256,12288]{1,0:T(8,128)(2,1)} %bitcast.27, bf16[256,12288]{1,0:T(8,128)(2,1)} %bitcast.28, ...), custom_call_target="tpu_custom_call" | custom-call | flops 10000000 | bytes 4000000 | tf_op jit(solution)/shard_map/edges/pallas_call | solution.py:131
  37.4 2.3 %collective-permute-start.2 = (bf16[144,4096]{1,0:T(8,128)(2,1)}, bf16[144,4096]{1,0:T(8,128)(2,1)}, u32[]{:S(2)}, u32[]{:S(2)}) collective-permute-start(bf16[144,4096]{1,0:T(8,128)(2,1)} %get-tuple-element.15), channel_id=1, source_target_pairs={{1,0},{2,1},{3,2},{4,3},{5,4},{6,5},{7,6},{8,7},{9,8},{10,9},{11,1... | collective-permute-start | bytes 3538952 | tf_op jit(solution)/shard_map/ppermute | solution.py:27
  39.7 3.3 %collective-permute-start.1 = (bf16[128,4096]{1,0:T(8,128)(2,1)}, bf16[128,4096]{1,0:T(8,128)(2,1)}, u32[]{:S(2)}, u32[]{:S(2)}) collective-permute-start(bf16[128,4096]{1,0:T(8,128)(2,1)} %get-tuple-element.14), channel_id=1, source_target_pairs={{0,1},{1,2},{2,3},{3,4},{4,5},{5,6},{6,7},{7,8},{8,9},{9,10},{10,1... | collective-permute-start | bytes 3145736 | tf_op jit(solution)/shard_map/ppermute | solution.py:27
  43.0 0.1 copy.16
  43.1 2.8 %copy-done = bf16[1,256,12288]{2,1,0:T(8,128)(2,1)S(1)} copy-done((bf16[1,256,12288]{2,1,0:T(8,128)(2,1)S(1)}, bf16[1,256,12288]{2,1,0:T(8,128)(2,1)}, u32[]{:S(2)}) %copy-start) | copy-done | bytes 6291480
  45.9 2.7 %gates.1 = (bf16[256,4096]{1,0:T(8,128)(2,1)S(1)}, bf16[256,4096]{1,0:T(8,128)(2,1)S(1)}) custom-call(bf16[256,12288]{1,0:T(8,128)(2,1)S(1)} %bitcast.35, f32[8,12288]{1,0:T(8,128)S(1)} %copy-done.2, bf16[256,4096]{1,0:T(8,128)(2,1)S(1)} %bitcast.38, f32[3,12288]{1,0:T(4,128)S(1)} %copy-done.3), custom_call_target="tpu_custom_call" | custom-call | flops 10000000 | bytes 8000000 | tf_op jit(solution)/shard_map/gates/pallas_call | solution.py:179
  48.6 2.2 %toeplitz_blocks.1 = (bf16[8192,256]{1,0:T(8,128)(2,1)S(1)}, bf16[8192,256]{1,0:T(8,128)(2,1)S(1)}) custom-call(f32[256,128]{1,0:T(8,128)S(1)} %reshape.53.filters_ref, bf16[128,128]{1,0:T(8,128)(2,1)S(1)} %copy-done.7), custom_call_target="tpu_custom_call" | custom-call | flops 1000000000 | bytes 10000000 | tf_op jit(solution)/shard_map/toeplitz_blocks/pallas_call | solution.py:74
  50.9 1.9 %copy-done.4 = bf16[8192,256]{1,0:T(8,128)(2,1)} copy-done((bf16[8192,256]{1,0:T(8,128)(2,1)}, bf16[8192,256]{1,0:T(8,128)(2,1)S(1)}, u32[]{:S(2)}) %copy-start.4) | copy-done | bytes 4194328
  52.8 2.0 %copy-done.5 = bf16[8192,256]{1,0:T(8,128)(2,1)} copy-done((bf16[8192,256]{1,0:T(8,128)(2,1)}, bf16[8192,256]{1,0:T(8,128)(2,1)S(1)}, u32[]{:S(2)}) %copy-start.5) | copy-done | bytes 4194328
  54.8 0.2 collective-permute-done.1.refs_4_
  55.0 0.2 collective-permute-done.2.refs_5_
  55.2 28.3 %hyena_main.1 = (bf16[256,4096]{1,0:T(8,128)(2,1)}, bf16[256,12288]{1,0:T(8,128)(2,1)}, f32[256,128]{1,0:T(8,128)S(1)}, f32[3,3,4096]{2,1,0:T(4,128)S(1)}) custom-call(bf16[256,12288]{1,0:T(8,128)(2,1)} %bitcast.32, bf16[256,12288]{1,0:T(8,128)(2,1)} %bitcast.33, bf16[256,12288]{1,0:T(8,128)(2,1)} %bitcast.34, bf16[256,4096]{1,0:T(8,128)(2,1)S(1)} %bitcast.39, ...), custom_call_target="tpu_custom_call" | custom-call | flops 10000000000 | bytes 20000000 | tf_op jit(solution)/shard_map/hyena_main/pallas_call | solution.py:341
  83.6 0.1 copy.17
  83.7 0.2 reshape.55
  83.9 0.1 copy.21
  84.1 0.2 copy.20
  84.3 21.5 %all_to_all.18 = f32[128,1,640]{2,1,0:T(1,128)S(1)} all-to-all(f32[128,1,640]{2,1,0:T(1,128)S(1)} %copy.20), channel_id=1, replica_groups=mesh['fsdp'=8,'ctx'=16] {'fsdp','ctx'}, dimensions={0} | all-to-all | bytes 655360 | tf_op jit(solution)/shard_map/all_to_all | solution.py:421
  105.8 0.2 reduce_sum.9
  106.1 0.6 slice.45
  106.7 0.1 slice.44
  106.8 0.6 pad_maximum_fusion
  (26 shorter events, 0.3 us)
Async XLA Ops:
  1.6 16.7 %collective-permute-start = (bf16[2,12288]{1,0:T(2,128)(2,1)S(1)}, bf16[2,12288]{1,0:T(2,128)(2,1)S(1)}, u32[]{:S(2)}, u32[]{:S(2)}) collective-permute-start(bf16[2,12288]{1,0:T(2,128)(2,1)S(1)} %slice_bitcast_fusion.1), channel_id=1, source_target_pairs={{0,1},{1,2},{2,3},{3,4},{4,5},{5,6},{6,7},{7,8},{8,9},{9,10},{10,1... | collective-permute-start | bytes 147464 | tf_op jit(solution)/shard_map/ppermute | solution.py:27
  8.5 21.7 %all-to-all-start = ((f32[128,1,640]{2,1,0:T(1,128)}), f32[128,1,640]{2,1,0:T(1,128)S(1)}, u32[]{:S(2)}, u32[]{:S(2)}) async-start(f32[128,1,640]{2,1,0:T(1,128)} %broadcast_in_dim.11), calls=%async_computation | async-start | bytes 655360 | tf_op jit(solution)/shard_map/all_to_all | solution.py:395
  31.5 11.7 %copy-start.1 = (bf16[1,256,4096]{2,1,0:T(8,128)(2,1)S(1)}, bf16[1,256,4096]{2,1,0:T(8,128)(2,1)}, u32[]{:S(2)}) copy-start(bf16[1,256,4096]{2,1,0:T(8,128)(2,1)} %param.6) | copy-start | bytes 6291460
  31.5 11.7 %copy-start.2 = (f32[8,12288]{1,0:T(8,128)S(1)}, f32[8,12288]{1,0:T(8,128)}, u32[]{:S(2)}) copy-start(f32[8,12288]{1,0:T(8,128)} %pad_convert_fusion.tail_a.tail_b.tail_c.refs_8_.refs_9_) | copy-start | bytes 1179652
  31.5 11.7 %copy-start.3 = (f32[3,12288]{1,0:T(4,128)S(1)}, f32[3,12288]{1,0:T(4,128)}, u32[]{:S(2)}) copy-start(f32[3,12288]{1,0:T(4,128)} %reshape.52.ta_ref.tb_ref.tc_ref.refs_10_.refs_11_.refs_12_) | copy-start | bytes 442372
  37.4 17.8 %collective-permute-start.2 = (bf16[144,4096]{1,0:T(8,128)(2,1)}, bf16[144,4096]{1,0:T(8,128)(2,1)}, u32[]{:S(2)}, u32[]{:S(2)}) collective-permute-start(bf16[144,4096]{1,0:T(8,128)(2,1)} %get-tuple-element.15), channel_id=1, source_target_pairs={{1,0},{2,1},{3,2},{4,3},{5,4},{6,5},{7,6},{8,7},{9,8},{10,9},{11,1... | collective-permute-start | bytes 3538952 | tf_op jit(solution)/shard_map/ppermute | solution.py:27
  39.7 15.3 %collective-permute-start.1 = (bf16[128,4096]{1,0:T(8,128)(2,1)}, bf16[128,4096]{1,0:T(8,128)(2,1)}, u32[]{:S(2)}, u32[]{:S(2)}) collective-permute-start(bf16[128,4096]{1,0:T(8,128)(2,1)} %get-tuple-element.14), channel_id=1, source_target_pairs={{0,1},{1,2},{2,3},{3,4},{4,5},{5,6},{6,7},{7,8},{8,9},{9,10},{10,1... | collective-permute-start | bytes 3145736 | tf_op jit(solution)/shard_map/ppermute | solution.py:27
  43.1 2.8 %copy-start = (bf16[1,256,12288]{2,1,0:T(8,128)(2,1)S(1)}, bf16[1,256,12288]{2,1,0:T(8,128)(2,1)}, u32[]{:S(2)}) copy-start(bf16[1,256,12288]{2,1,0:T(8,128)(2,1)} %param.5) | copy-start | bytes 18874372
  45.9 2.7 %copy-start.7 = (bf16[128,128]{1,0:T(8,128)(2,1)S(1)}, bf16[128,128]{1,0:T(8,128)(2,1)}, u32[]{:S(2)}) copy-start(bf16[128,128]{1,0:T(8,128)(2,1)} %constant.10.clone.turn_ref) | copy-start | bytes 98308
  48.6 6.6 %copy-start.6 = (bf16[256,4096]{1,0:T(8,128)(2,1)}, bf16[256,4096]{1,0:T(8,128)(2,1)S(1)}, u32[]{:S(2)}) copy-start(bf16[256,4096]{1,0:T(8,128)(2,1)S(1)} %get-tuple-element.17.refs_7_) | copy-start | bytes 6291460
  50.9 2.0 %copy-start.4 = (bf16[8192,256]{1,0:T(8,128)(2,1)}, bf16[8192,256]{1,0:T(8,128)(2,1)S(1)}, u32[]{:S(2)}) copy-start(bf16[8192,256]{1,0:T(8,128)(2,1)S(1)} %get-tuple-element.18.refs_13_) | copy-start | bytes 12582916
  52.8 2.0 %copy-start.5 = (bf16[8192,256]{1,0:T(8,128)(2,1)}, bf16[8192,256]{1,0:T(8,128)(2,1)S(1)}, u32[]{:S(2)}) copy-start(bf16[8192,256]{1,0:T(8,128)(2,1)S(1)} %get-tuple-element.19.refs_14_) | copy-start | bytes 12582916
